TPU v7x, 512 devices: a whole 4x8x8 slice. The times are simulated.
512 devices in a mesh: chan: 64 (over z, x, core), seg: 8 (over y).
Axes of the slice: x: 4, y: 8, z: 8, core: 2. Of those that a mesh axis runs over, the one named last changes fastest.
Arguments:
- raw: bfloat16 [16, 8192, 1536], P('seg', 'chan'), may hold values from -300 to 300, as said below
- send_order: int32 [8192], P('chan'), may hold values from 0 to 127, as said below
- pair_first: int32 [16384], P('chan'), may hold values from 0 to 127, as said below
- pair_offset: int32 [16384], P('chan'), may hold values from 1 to 48
- pair_count: int32 [64], P('chan'), may hold values from 32 to 256, as said below
Outputs:
- stacks: float32 [16384, 256], P(('chan', 'seg'))
Inputs may be any that keep to these rules, and one draw needn't show every extreme that they name: `send_order`: on each index p of chan the 128 entries are a permutation of 0 .. 127, the local stored channels; entries b * 2 .. b * 2 + 1 go to pair block b. `pair_first`: a position inside the owner's block; in the last block pair_first + pair_offset stays below 128, so a pair's second channel lies in its own block or the next. `pair_count`: some block is full in every draw. `raw`: channels differ in gain and spectral colour.
All inputs are finite; a program needn't handle non-finite values.
Results may differ from a plain program's by a relative error of at most 0.0077.
Values may be sent and summed in bfloat16 or wider, within the bound.
No kernel may reach another device: no remote copies, remote signals or barrier semaphores. Data moves between devices by JAX's collectives and lax.ppermute only.
A program may use at most 64 MiB of HBM per device.

v0:
```python
import math

import jax
import jax.numpy as jnp
import numpy as np
from jax import lax
from jax.experimental import pallas as pl
from jax.experimental.pallas import tpu as pltpu
from jax.sharding import PartitionSpec as P

L = 1536
F = 512
BAND = 32
LAGS = 256
REACH = 48
COLS = 256
STEPS = 4
BF = jnp.bfloat16
F32 = jnp.float32


def forward_table():
    bins = 1 + np.arange(F)
    samples = np.arange(L)
    phase = (samples[:, None] * bins[None, :] % L).astype(np.float32) * np.float32(2.0 * math.pi / L)
    cosines = np.cos(phase).astype(BF).reshape(L, STEPS, F // STEPS)
    sines = (-np.sin(phase)).astype(BF).reshape(L, STEPS, F // STEPS)
    return np.ascontiguousarray(np.concatenate([cosines, sines], axis=-1).transpose(1, 0, 2))


def band_tables():
    bin_index = np.arange(F)
    nearby = np.abs(bin_index[:, None] - bin_index[None, :]) <= BAND
    return nearby.astype(BF), (1.0 / nearby.sum(axis=0, keepdims=True)).astype(np.float32)


def inverse_tables(factor):
    bins = 1 + np.arange(F)
    lag_shift = np.arange(LAGS) - LAGS // 2
    phase = (bins[:, None] * lag_shift[None, :] % L).astype(np.float64) * (2.0 * math.pi / L)
    table = (np.concatenate([np.cos(phase), -np.sin(phase)], axis=0) * factor).astype(np.float32)
    high = table.astype(BF)
    return high, (table - high.astype(np.float32)).astype(BF)


def dot(a, b):
    return jnp.dot(a, b, preferred_element_type=F32)


def spread_matrix(blocks, back):
    rows = blocks * 16
    r = lax.broadcasted_iota(jnp.int32, (rows, rows), 0)
    k = lax.broadcasted_iota(jnp.int32, (rows, rows), 1)
    mixed, apart = (k, r) if back else (r, k)
    p, cs, j = mixed // 16, (mixed % 16) // 2, mixed % 2
    return (apart == cs * (2 * blocks) + p * 2 + j).astype(F32).astype(BF)


def whiten_kernel(raw_ref, order_ref, table_ref, band_ref, inv_ref, out_ref, normed, real, imag, smooth):
    step = pl.program_id(0)
    width = F // STEPS

    @pl.when(step == 0)
    def _():
        wave = raw_ref[...].astype(F32)
        mean = jnp.sum(wave * wave, axis=-1, keepdims=True) * (1.0 / L)
        normed[...] = (wave * lax.rsqrt(mean + 1e-05)).astype(BF)
        smooth[...] = jnp.zeros_like(smooth)

    spec = dot(normed[...], table_ref[0])
    re, im = spec[:, :width], spec[:, width:]
    real[step] = re
    imag[step] = im
    power = re * re + im * im
    high = power.astype(BF)
    low = (power - high.astype(F32)).astype(BF)
    near = band_ref[...]
    smooth[...] += dot(high, near) + dot(low, near)

    @pl.when(step == STEPS - 1)
    def _():
        factor = lax.rsqrt(smooth[...] * inv_ref[...] + 1e-06)
        channels = lax.broadcasted_iota(jnp.int32, (128, 128), 0)
        pick = (channels == order_ref[...]).astype(F32).T.astype(BF)
        picked = []
        for s in range(2):
            rows = slice(s * 128, s * 128 + 128)
            parts = [real[i, rows] * factor[rows, i * width : (i + 1) * width] for i in range(STEPS)]
            parts += [imag[i, rows] * factor[rows, i * width : (i + 1) * width] for i in range(STEPS)]
            white = jnp.concatenate(parts, axis=1).astype(BF)
            picked.append(dot(pick, white).astype(BF))
        mix = spread_matrix(16, False)
        for b in range(4):
            stacked = jnp.concatenate(
                [
                    picked[s][b * 32 : b * 32 + 32, c * COLS : (c + 1) * COLS]
                    for c in range(4)
                    for s in range(2)
                ],
                axis=0,
            )
            out_ref[b * 16 : b * 16 + 16] = dot(mix, stacked).astype(BF).reshape(16, 16, COLS)


def whitened(raw, send_order):
    near, inv = band_tables()
    return pl.pallas_call(
        whiten_kernel,
        grid=(STEPS,),
        in_specs=[
            pl.BlockSpec((256, L), lambda i: (0, 0)),
            pl.BlockSpec((1, 128), lambda i: (0, 0)),
            pl.BlockSpec((1, L, COLS), lambda i: (i, 0, 0)),
            pl.BlockSpec((F // STEPS, F), lambda i: (i, 0)),
            pl.BlockSpec((1, F), lambda i: (0, 0)),
        ],
        out_specs=pl.BlockSpec((64, 16, COLS), lambda i: (0, 0, 0)),
        out_shape=jax.ShapeDtypeStruct((64, 16, COLS), BF),
        scratch_shapes=[
            pltpu.VMEM((256, L), BF),
            pltpu.VMEM((STEPS, 256, F // STEPS), F32),
            pltpu.VMEM((STEPS, 256, F // STEPS), F32),
            pltpu.VMEM((256, F), F32),
        ],
        compiler_params=pltpu.CompilerParams(vmem_limit_bytes=32 * 1024 * 1024),
        name="whiten",
    )(raw.reshape(256, L), send_order.reshape(1, 128), forward_table(), near, inv)


def pairs_kernel(own_ref, rim_ref, first_ref, offset_ref, count_ref, high_ref, low_ref, out_ref, rows_ref):
    apart = spread_matrix(16, True)
    for b in range(4):
        block = dot(apart, own_ref[b * 16 : b * 16 + 16].reshape(256, COLS)).astype(BF)
        for c in range(4):
            for s in range(2):
                at = (c * 2 + s) * 32
                rows_ref[s, c, b * 32 : b * 32 + 32] = block[at : at + 32]
    apart = spread_matrix(8, True)
    for b in range(3):
        block = dot(apart, rim_ref[b * 8 : b * 8 + 8].reshape(128, COLS)).astype(BF)
        for c in range(4):
            for s in range(2):
                at = (c * 2 + s) * 16
                rows_ref[s, c, 128 + b * 16 : 128 + b * 16 + 16] = block[at : at + 16]
    first = first_ref[...]
    second = first + offset_ref[...]
    slot = lax.broadcasted_iota(jnp.int32, (1, 256), 1)
    first = jnp.where(slot < count_ref[0], first, -1)
    left_at = lax.broadcasted_iota(jnp.int32, (128, 256), 0)
    left_pick = (left_at == first).astype(F32).T.astype(BF)
    right_at = lax.broadcasted_iota(jnp.int32, (176, 256), 0)
    right_pick = (right_at == second).astype(F32).T.astype(BF)
    total = jnp.zeros((256, LAGS), F32)
    for c in range(2):
        re = jnp.zeros((256, COLS), F32)
        im = jnp.zeros((256, COLS), F32)
        for s in range(2):
            a_re = dot(left_pick, rows_ref[s, c, :128])
            a_im = dot(left_pick, rows_ref[s, c + 2, :128])
            c_re = dot(right_pick, rows_ref[s, c])
            c_im = dot(right_pick, rows_ref[s, c + 2])
            re += a_re * c_re + a_im * c_im
            im += a_im * c_re - a_re * c_im
        for part, row in ((re, c * COLS), (im, (c + 2) * COLS)):
            high = part.astype(BF)
            low = (part - high.astype(F32)).astype(BF)
            table = high_ref[row : row + COLS]
            total += dot(high, table) + dot(low, table) + dot(high, low_ref[row : row + COLS])
    out_ref[...] = total.astype(BF)


def pair_lags(own, rim, pair_first, pair_offset, pair_count, factor):
    high, low = inverse_tables(factor)
    vmem = pl.BlockSpec(memory_space=pltpu.VMEM)
    return pl.pallas_call(
        pairs_kernel,
        in_specs=[vmem, vmem, vmem, vmem, pl.BlockSpec(memory_space=pltpu.SMEM), vmem, vmem],
        out_specs=vmem,
        out_shape=jax.ShapeDtypeStruct((256, LAGS), BF),
        scratch_shapes=[pltpu.VMEM((2, 4, 176, COLS), BF)],
        compiler_params=pltpu.CompilerParams(vmem_limit_bytes=32 * 1024 * 1024),
        name="pairs",
    )(own, rim, pair_first.reshape(1, 256), pair_offset.reshape(1, 256), pair_count, high, low)


def on_device(raw, send_order, pair_first, pair_offset, pair_count):
    seg_count = raw.shape[0]
    groups = lax.axis_size("seg")
    blocks = lax.axis_size("chan")
    sent = whitened(raw, send_order)
    own = lax.all_to_all(sent, "chan", split_axis=0, concat_axis=0, tiled=True)
    rim = lax.ppermute(own[: REACH // 2], "chan", [(i + 1, i) for i in range(blocks - 1)])
    lags = pair_lags(own, rim, pair_first, pair_offset, pair_count, 1.0 / math.sqrt(seg_count * groups * F))
    shares = lax.all_to_all(lags.reshape(groups, 256 // groups, LAGS), "seg", 0, 0, tiled=True)
    return jnp.sum(shares.astype(F32), axis=0)


def solution(mesh):
    return jax.shard_map(
        on_device,
        mesh=mesh,
        in_specs=(P("seg", "chan", None), P("chan"), P("chan"), P("chan"), P("chan")),
        out_specs=P(("chan", "seg"), None),
        check_vma=False,
    )
```

profile of v0, /device:TPU:5, one launch (start us, length us, event | category | flops | bytes accessed | tf_op | source)
XLA Modules:
  0.0 66.4 jit_solution(14322072671813152151)
XLA Ops:
  0.0 0.0 copy-start
  0.0 1.9 %copy-done = bf16[4,1536,256]{2,1,0:T(8,128)(2,1)S(1)} copy-done((bf16[4,1536,256]{2,1,0:T(8,128)(2,1)S(1)}, bf16[4,1536,256]{2,1,0:T(8,128)(2,1)}, u32[]{:S(2)}) %copy-start) | copy-done | bytes 3145752
  1.9 0.0 copy-start.1
  1.9 1.1 %copy-done.1 = bf16[2,128,1536]{2,1,0:T(8,128)(2,1)S(1)} copy-done((bf16[2,128,1536]{2,1,0:T(8,128)(2,1)S(1)}, bf16[2,128,1536]{2,1,0:T(8,128)(2,1)}, u32[]{:S(2)}) %copy-start.1) | copy-done | bytes 786456
  3.0 0.0 copy-start.4
  3.0 1.0 %copy-done.4 = bf16[512,512]{1,0:T(8,128)(2,1)S(1)} copy-done((bf16[512,512]{1,0:T(8,128)(2,1)S(1)}, bf16[512,512]{1,0:T(8,128)(2,1)}, u32[]{:S(2)}) %copy-start.4) | copy-done | bytes 524312
  4.1 0.0 copy-start.5
  4.1 0.7 %copy-done.5 = f32[1,512]{1,0:T(1,128)S(1)} copy-done((f32[1,512]{1,0:T(1,128)S(1)}, f32[1,512]{1,0:T(1,128)}, u32[]{:S(2)}) %copy-start.5) | copy-done | bytes 2072
  4.7 0.0 copy-start.8
  4.8 0.7 copy-done.8
  5.4 0.0 copy-start.2
  5.4 0.0 copy-start.3
  5.4 0.0 copy-start.6
  5.4 0.0 copy-start.7
  5.4 4.2 %whiten.1 = bf16[64,16,256]{2,1,0:T(8,128)(2,1)S(1)} custom-call(bf16[256,1536]{1,0:T(8,128)(2,1)S(1)} %bitcast.5, s32[1,128]{1,0:T(1,128)S(1)} %bitcast.9, bf16[4,1536,256]{2,1,0:T(8,128)(2,1)S(1)} %copy-done, bf16[512,512]{1,0:T(8,128)(2,1)S(1)} %copy-done.4, f32[1,512]{1,0:T(1,128)S(1)} %copy-done.5), custom_call_target="tpu_custom_call" | custom-call | tf_op jit(solution)/shard_map/whiten/pallas_call | solution.py:107
  9.7 30.7 %all_to_all.10.own_ref = bf16[64,16,256]{2,1,0:T(8,128)(2,1)S(1)} all-to-all(bf16[64,16,256]{2,1,0:T(8,128)(2,1)S(1)} %whiten.1), channel_id=1, replica_groups=mesh['chan'=64,'seg'=8] {'chan'}, dimensions={0} | all-to-all | bytes 1048576 | tf_op jit(solution)/shard_map/all_to_all | solution.py:191
  40.4 3.1 %collective-permute-start = (bf16[24,16,256]{2,1,0:T(8,128)(2,1)S(1)}, bf16[24,16,256]{2,1,0:T(8,128)(2,1)S(1)}, u32[]{:S(2)}, u32[]{:S(2)}) collective-permute-start(bf16[24,16,256]{2,1,0:T(8,128)(2,1)S(1)} %slice.4), channel_id=1, source_target_pairs={{8,0},{16,8},{24,16},{32,24},{40,32},{48,40},{56,48},{64,56},{72,6... | collective-permute-start | bytes 589832 | tf_op jit(solution)/shard_map/ppermute | solution.py:192
  44.1 3.5 %collective-permute-done.rim_ref = bf16[24,16,256]{2,1,0:T(8,128)(2,1)S(1)} collective-permute-done((bf16[24,16,256]{2,1,0:T(8,128)(2,1)S(1)}, bf16[24,16,256]{2,1,0:T(8,128)(2,1)S(1)}, u32[]{:S(2)}, u32[]{:S(2)}) %collective-permute-start) | collective-permute-done | bytes 196640 | tf_op jit(solution)/shard_map/ppermute | solution.py:192
  47.6 0.0 copy-done.2
  47.6 0.0 copy-done.3
  47.6 0.0 copy-done.6
  47.6 0.0 copy-done.7
  47.6 2.0 %pairs.1 = bf16[256,256]{1,0:T(8,128)(2,1)S(1)} custom-call(bf16[64,16,256]{2,1,0:T(8,128)(2,1)S(1)} %all_to_all.10.own_ref, bf16[24,16,256]{2,1,0:T(8,128)(2,1)S(1)} %collective-permute-done.rim_ref, s32[1,256]{1,0:T(1,128)S(1)} %bitcast.7, s32[1,256]{1,0:T(1,128)S(1)} %bitcast.8, s32[1]{0:T(128)S(6)} %copy.11.count_ref, bf16[1024,256]{1,0:T(8,128)(2,1)S(1)} %copy-done.2, ...), custom_call_target="tpu_custom_call" | custom-call | tf_op jit(solution)/shard_map/pairs/pallas_call | solution.py:175
  49.6 16.2 %all_to_all.11 = bf16[8,32,256]{2,1,0:T(8,128)(2,1)S(1)} all-to-all(bf16[8,32,256]{2,1,0:T(8,128)(2,1)S(1)} %bitcast.6), channel_id=1, replica_groups=mesh['chan'=64,'seg'=8] {'seg'}, dimensions={0} | all-to-all | bytes 262144 | tf_op jit(solution)/shard_map/all_to_all | solution.py:194
  65.8 0.6 convert_reduce_fusion
  (1 shorter events, 0.0 us)
Async XLA Ops:
  0.0 1.9 %copy-start = (bf16[4,1536,256]{2,1,0:T(8,128)(2,1)S(1)}, bf16[4,1536,256]{2,1,0:T(8,128)(2,1)}, u32[]{:S(2)}) copy-start(bf16[4,1536,256]{2,1,0:T(8,128)(2,1)} %constant.12.clone.table_ref) | copy-start | bytes 9437188
  1.9 1.1 %copy-start.1 = (bf16[2,128,1536]{2,1,0:T(8,128)(2,1)S(1)}, bf16[2,128,1536]{2,1,0:T(8,128)(2,1)}, u32[]{:S(2)}) copy-start(bf16[2,128,1536]{2,1,0:T(8,128)(2,1)} %param.10) | copy-start | bytes 2359300
  3.0 1.0 %copy-start.4 = (bf16[512,512]{1,0:T(8,128)(2,1)S(1)}, bf16[512,512]{1,0:T(8,128)(2,1)}, u32[]{:S(2)}) copy-start(bf16[512,512]{1,0:T(8,128)(2,1)} %constant.13.clone.band_ref) | copy-start | bytes 1572868
  4.1 0.7 %copy-start.5 = (f32[1,512]{1,0:T(1,128)S(1)}, f32[1,512]{1,0:T(1,128)}, u32[]{:S(2)}) copy-start(f32[1,512]{1,0:T(1,128)} %constant.14.clone.inv_ref) | copy-start | bytes 6148
  4.7 0.7 copy-start.8
  5.4 42.2 %copy-start.2 = (bf16[1024,256]{1,0:T(8,128)(2,1)S(1)}, bf16[1024,256]{1,0:T(8,128)(2,1)}, u32[]{:S(2)}) copy-start(bf16[1024,256]{1,0:T(8,128)(2,1)} %constant.15.clone.high_ref) | copy-start | bytes 1572868
  5.4 42.2 %copy-start.3 = (bf16[1024,256]{1,0:T(8,128)(2,1)S(1)}, bf16[1024,256]{1,0:T(8,128)(2,1)}, u32[]{:S(2)}) copy-start(bf16[1024,256]{1,0:T(8,128)(2,1)} %constant.16.clone.low_ref) | copy-start | bytes 1572868
  5.4 42.2 %copy-start.6 = (s32[256]{0:T(256)S(1)}, s32[256]{0:T(256)}, u32[]{:S(2)}) copy-start(s32[256]{0:T(256)} %param.12) | copy-start | bytes 3076
  5.4 42.2 %copy-start.7 = (s32[256]{0:T(256)S(1)}, s32[256]{0:T(256)}, u32[]{:S(2)}) copy-start(s32[256]{0:T(256)} %param.13) | copy-start | bytes 3076
  40.4 7.2 %collective-permute-start = (bf16[24,16,256]{2,1,0:T(8,128)(2,1)S(1)}, bf16[24,16,256]{2,1,0:T(8,128)(2,1)S(1)}, u32[]{:S(2)}, u32[]{:S(2)}) collective-permute-start(bf16[24,16,256]{2,1,0:T(8,128)(2,1)S(1)} %slice.4), channel_id=1, source_target_pairs={{8,0},{16,8},{24,16},{32,24},{40,32},{48,40},{56,48},{64,56},{72,6... | collective-permute-start | bytes 589832 | tf_op jit(solution)/shard_map/ppermute | solution.py:192
where the time goes:
time: 66.8 us; the launch traced here: 66.4 us
  blocking collectives  46.9 us (70%)
  Pallas kernels  6.21 us (9%)
  local copies, waits for them, and re-layouts  5.43 us (8%)
  waiting for transfers between devices  3.48 us (5%)
  starting transfers between devices  3.07 us (5%)
  between operations  0.7 us (1%)
    all_to_all x1, blocking collectives, on_device(): own = lax.all_to_all(sent, 'chan', split_axis=0, concat_axis=0, tiled=True)  30.7 us
    all_to_all x1, blocking collectives, on_device(): lax.all_to_all(lags.reshape(groups, 256 // groups, LAGS), 'seg', 0, 0, ti...  16.2 us
    unnamed x18, local copies, waits for them, and re-layouts  5.41 us
    pallas_call x1, Pallas kernels, whitened(): pl.pallas_call(whiten_kernel, grid=(STEPS,), in_specs=[pl.BlockSpec((256,...  4.24 us
    ppermute x1, waiting for transfers between devices, on_device(): lax.ppermute(own[:REACH // 2], 'chan', [(i + 1, i) for i in range(blocks...  3.48 us
    ppermute x1, starting transfers between devices, on_device(): lax.ppermute(own[:REACH // 2], 'chan', [(i + 1, i) for i in range(blocks...  3.07 us
    pallas_call x1, Pallas kernels, pair_lags(): pl.pallas_call(pairs_kernel, in_specs=[vmem, vmem, vmem, vmem, pl.BlockSp...  1.97 us
  transfers between devices with their start and end apart: 1, of which 1 were waited for; matrix products, arithmetic and copies ran while one was open for 0% of the time, Pallas kernels for 0%

commit v1 on v0

--- a/solution.py
+++ b/solution.py
@@ -56,75 +56,79 @@
     return (apart == cs * (2 * blocks) + p * 2 + j).astype(F32).astype(BF)
 
 
-def whiten_kernel(raw_ref, order_ref, table_ref, band_ref, inv_ref, out_ref, normed, real, imag, smooth):
-    step = pl.program_id(0)
+def whiten_kernel(
+    raw_hbm, order_hbm, table_hbm, band_hbm, inv_hbm, out_ref, raw_ref, order_ref, table_ref, band_ref, inv_ref, normed, sems
+):
     width = F // STEPS
-
-    @pl.when(step == 0)
-    def _():
-        wave = raw_ref[...].astype(F32)
+    half = F // 2
+    copies = [pltpu.make_async_copy(raw_hbm.at[s], raw_ref.at[s], sems.at[s]) for s in range(2)]
+    copies += [pltpu.make_async_copy(table_hbm.at[i], table_ref.at[i], sems.at[2 + i]) for i in range(STEPS)]
+    copies += [
+        pltpu.make_async_copy(band_hbm, band_ref, sems.at[2 + STEPS]),
+        pltpu.make_async_copy(inv_hbm, inv_ref, sems.at[3 + STEPS]),
+        pltpu.make_async_copy(order_hbm, order_ref, sems.at[4 + STEPS]),
+    ]
+    for copy in copies:
+        copy.start()
+    mix = spread_matrix(16, False)
+    for s in range(2):
+        copies[s].wait()
+        wave = raw_ref[s].astype(F32)
         mean = jnp.sum(wave * wave, axis=-1, keepdims=True) * (1.0 / L)
-        normed[...] = (wave * lax.rsqrt(mean + 1e-05)).astype(BF)
-        smooth[...] = jnp.zeros_like(smooth)
-
-    spec = dot(normed[...], table_ref[0])
-    re, im = spec[:, :width], spec[:, width:]
-    real[step] = re
-    imag[step] = im
-    power = re * re + im * im
-    high = power.astype(BF)
-    low = (power - high.astype(F32)).astype(BF)
-    near = band_ref[...]
-    smooth[...] += dot(high, near) + dot(low, near)
-
-    @pl.when(step == STEPS - 1)
-    def _():
-        factor = lax.rsqrt(smooth[...] * inv_ref[...] + 1e-06)
-        channels = lax.broadcasted_iota(jnp.int32, (128, 128), 0)
-        pick = (channels == order_ref[...]).astype(F32).T.astype(BF)
-        picked = []
-        for s in range(2):
-            rows = slice(s * 128, s * 128 + 128)
-            parts = [real[i, rows] * factor[rows, i * width : (i + 1) * width] for i in range(STEPS)]
-            parts += [imag[i, rows] * factor[rows, i * width : (i + 1) * width] for i in range(STEPS)]
-            white = jnp.concatenate(parts, axis=1).astype(BF)
-            picked.append(dot(pick, white).astype(BF))
-        mix = spread_matrix(16, False)
-        for b in range(4):
-            stacked = jnp.concatenate(
-                [
-                    picked[s][b * 32 : b * 32 + 32, c * COLS : (c + 1) * COLS]
-                    for c in range(4)
-                    for s in range(2)
-                ],
-                axis=0,
-            )
-            out_ref[b * 16 : b * 16 + 16] = dot(mix, stacked).astype(BF).reshape(16, 16, COLS)
+        normed[s * 128 : s * 128 + 128] = (wave * lax.rsqrt(mean + 1e-05)).astype(BF)
+    real, imag = [], []
+    smooth = None
+    for i in range(STEPS):
+        copies[2 + i].wait()
+        spec = dot(normed[...], table_ref[i])
+        real.append(spec[:, :width])
+        imag.append(spec[:, width:])
+        if i == 1:
+            copies[2 + STEPS].wait()
+        if i % 2:
+            power = jnp.concatenate([real[k] * real[k] + imag[k] * imag[k] for k in (i - 1, i)], axis=1)
+            high = power.astype(BF)
+            low = (power - high.astype(F32)).astype(BF)
+            near = band_ref[(i // 2) * half : (i // 2 + 1) * half]
+            part = dot(high, near) + dot(low, near)
+            smooth = part if smooth is None else smooth + part
+    for copy in copies[3 + STEPS :]:
+        copy.wait()
+    factor = lax.rsqrt(smooth * inv_ref[...] + 1e-06)
+    channels = lax.broadcasted_iota(jnp.int32, (128, 128), 0)
+    pick = (channels == order_ref[...]).astype(F32).T.astype(BF)
+    picked = []
+    for s in range(2):
+        rows = slice(s * 128, s * 128 + 128)
+        scaled = [x[i][rows] * factor[rows, i * width : (i + 1) * width] for x in (real, imag) for i in range(STEPS)]
+        picked.append(dot(pick, jnp.concatenate(scaled, axis=1).astype(BF)).astype(BF))
+    for b in range(4):
+        stacked = jnp.concatenate(
+            [picked[s][b * 32 : b * 32 + 32, c * COLS : (c + 1) * COLS] for c in range(4) for s in range(2)], axis=0
+        )
+        out_ref[b * 16 : b * 16 + 16] = dot(mix, stacked).astype(BF).reshape(16, 16, COLS)
 
 
 def whitened(raw, send_order):
     near, inv = band_tables()
+    hbm = pl.BlockSpec(memory_space=pltpu.HBM)
     return pl.pallas_call(
         whiten_kernel,
-        grid=(STEPS,),
-        in_specs=[
-            pl.BlockSpec((256, L), lambda i: (0, 0)),
-            pl.BlockSpec((1, 128), lambda i: (0, 0)),
-            pl.BlockSpec((1, L, COLS), lambda i: (i, 0, 0)),
-            pl.BlockSpec((F // STEPS, F), lambda i: (i, 0)),
-            pl.BlockSpec((1, F), lambda i: (0, 0)),
-        ],
-        out_specs=pl.BlockSpec((64, 16, COLS), lambda i: (0, 0, 0)),
+        in_specs=[hbm] * 5,
+        out_specs=pl.BlockSpec(memory_space=pltpu.VMEM),
         out_shape=jax.ShapeDtypeStruct((64, 16, COLS), BF),
         scratch_shapes=[
+            pltpu.VMEM((2, 128, L), BF),
+            pltpu.VMEM((1, 128), jnp.int32),
+            pltpu.VMEM((STEPS, L, COLS), BF),
+            pltpu.VMEM((F, F), BF),
+            pltpu.VMEM((1, F), F32),
             pltpu.VMEM((256, L), BF),
-            pltpu.VMEM((STEPS, 256, F // STEPS), F32),
-            pltpu.VMEM((STEPS, 256, F // STEPS), F32),
-            pltpu.VMEM((256, F), F32),
+            pltpu.SemaphoreType.DMA((5 + STEPS,)),
         ],
         compiler_params=pltpu.CompilerParams(vmem_limit_bytes=32 * 1024 * 1024),
         name="whiten",
-    )(raw.reshape(256, L), send_order.reshape(1, 128), forward_table(), near, inv)
+    )(raw, send_order.reshape(1, 128), forward_table(), near, inv)
 
 
 def pairs_kernel(own_ref, rim_ref, first_ref, offset_ref, count_ref, high_ref, low_ref, out_ref, rows_ref):

time: 66.8 us -> 66.9 us (level)
  no operation moved by 1% of the time
where the time goes in v1:
time: 66.9 us; the launch traced here: 66.5 us
  blocking collectives  46.9 us (70%)
  Pallas kernels  6.34 us (9%)
  local copies, waits for them, and re-layouts  5.43 us (8%)
  waiting for transfers between devices  3.48 us (5%)
  starting transfers between devices  3.07 us (5%)
  between operations  0.7 us (1%)
    all_to_all x1, blocking collectives, on_device(): own = lax.all_to_all(sent, 'chan', split_axis=0, concat_axis=0, tiled=True)  30.7 us
    all_to_all x1, blocking collectives, on_device(): lax.all_to_all(lags.reshape(groups, 256 // groups, LAGS), 'seg', 0, 0, ti...  16.2 us
    unnamed x18, local copies, waits for them, and re-layouts  5.41 us
    pallas_call x1, Pallas kernels, whitened(): pl.pallas_call(whiten_kernel, in_specs=[hbm] * 5, out_specs=pl.BlockSpec(...  4.37 us
    ppermute x1, waiting for transfers between devices, on_device(): lax.ppermute(own[:REACH // 2], 'chan', [(i + 1, i) for i in range(blocks...  3.48 us
    ppermute x1, starting transfers between devices, on_device(): lax.ppermute(own[:REACH // 2], 'chan', [(i + 1, i) for i in range(blocks...  3.07 us
    pallas_call x1, Pallas kernels, pair_lags(): pl.pallas_call(pairs_kernel, in_specs=[vmem, vmem, vmem, vmem, pl.BlockSp...  1.97 us
  transfers between devices with their start and end apart: 1, of which 1 were waited for; matrix products, arithmetic and copies ran while one was open for 0% of the time, Pallas kernels for 0%

profile of v1, /device:TPU:5, one launch (start us, length us, event | category | flops | bytes accessed | tf_op | source)
XLA Modules:
  0.0 66.5 jit_solution(14274181175282366061)
XLA Ops:
  0.0 0.0 copy-start
  0.0 1.9 %copy-done = bf16[4,1536,256]{2,1,0:T(8,128)(2,1)S(1)} copy-done((bf16[4,1536,256]{2,1,0:T(8,128)(2,1)S(1)}, bf16[4,1536,256]{2,1,0:T(8,128)(2,1)}, u32[]{:S(2)}) %copy-start) | copy-done | bytes 3145752
  1.9 0.0 copy-start.1
  1.9 1.1 %copy-done.1 = bf16[2,128,1536]{2,1,0:T(8,128)(2,1)S(1)} copy-done((bf16[2,128,1536]{2,1,0:T(8,128)(2,1)S(1)}, bf16[2,128,1536]{2,1,0:T(8,128)(2,1)}, u32[]{:S(2)}) %copy-start.1) | copy-done | bytes 786456
  3.0 0.0 copy-start.4
  3.0 1.0 %copy-done.4 = bf16[512,512]{1,0:T(8,128)(2,1)S(1)} copy-done((bf16[512,512]{1,0:T(8,128)(2,1)S(1)}, bf16[512,512]{1,0:T(8,128)(2,1)}, u32[]{:S(2)}) %copy-start.4) | copy-done | bytes 524312
  4.1 0.0 copy-start.5
  4.1 0.7 %copy-done.5 = f32[1,512]{1,0:T(1,128)S(1)} copy-done((f32[1,512]{1,0:T(1,128)S(1)}, f32[1,512]{1,0:T(1,128)}, u32[]{:S(2)}) %copy-start.5) | copy-done | bytes 2072
  4.7 0.0 copy-start.8
  4.8 0.7 copy-done.8
  5.4 0.0 copy-start.2
  5.4 0.0 copy-start.3
  5.4 0.0 copy-start.6
  5.4 0.0 copy-start.7
  5.4 4.4 %whiten.1 = bf16[64,16,256]{2,1,0:T(8,128)(2,1)S(1)} custom-call(bf16[2,128,1536]{2,1,0:T(8,128)(2,1)S(1)} %copy-done.1, s32[1,128]{1,0:T(1,128)S(1)} %bitcast.7, bf16[4,1536,256]{2,1,0:T(8,128)(2,1)S(1)} %copy-done, bf16[512,512]{1,0:T(8,128)(2,1)S(1)} %copy-done.4, f32[1,512]{1,0:T(1,128)S(1)} %copy-done.5), custom_call_target="tpu_custom_call" | custom-call | tf_op jit(solution)/shard_map/whiten/pallas_call | solution.py:115
  9.8 30.7 %all_to_all.10.own_ref = bf16[64,16,256]{2,1,0:T(8,128)(2,1)S(1)} all-to-all(bf16[64,16,256]{2,1,0:T(8,128)(2,1)S(1)} %whiten.1), channel_id=1, replica_groups=mesh['chan'=64,'seg'=8] {'chan'}, dimensions={0} | all-to-all | bytes 1048576 | tf_op jit(solution)/shard_map/all_to_all | solution.py:195
  40.5 3.1 %collective-permute-start = (bf16[24,16,256]{2,1,0:T(8,128)(2,1)S(1)}, bf16[24,16,256]{2,1,0:T(8,128)(2,1)S(1)}, u32[]{:S(2)}, u32[]{:S(2)}) collective-permute-start(bf16[24,16,256]{2,1,0:T(8,128)(2,1)S(1)} %slice.4), channel_id=1, source_target_pairs={{8,0},{16,8},{24,16},{32,24},{40,32},{48,40},{56,48},{64,56},{72,6... | collective-permute-start | bytes 589832 | tf_op jit(solution)/shard_map/ppermute | solution.py:196
  44.3 3.5 %collective-permute-done.rim_ref = bf16[24,16,256]{2,1,0:T(8,128)(2,1)S(1)} collective-permute-done((bf16[24,16,256]{2,1,0:T(8,128)(2,1)S(1)}, bf16[24,16,256]{2,1,0:T(8,128)(2,1)S(1)}, u32[]{:S(2)}, u32[]{:S(2)}) %collective-permute-start) | collective-permute-done | bytes 196640 | tf_op jit(solution)/shard_map/ppermute | solution.py:196
  47.7 0.0 copy-done.2
  47.7 0.0 copy-done.3
  47.7 0.0 copy-done.6
  47.7 0.0 copy-done.7
  47.8 2.0 %pairs.1 = bf16[256,256]{1,0:T(8,128)(2,1)S(1)} custom-call(bf16[64,16,256]{2,1,0:T(8,128)(2,1)S(1)} %all_to_all.10.own_ref, bf16[24,16,256]{2,1,0:T(8,128)(2,1)S(1)} %collective-permute-done.rim_ref, s32[1,256]{1,0:T(1,128)S(1)} %bitcast.5, s32[1,256]{1,0:T(1,128)S(1)} %bitcast.6, s32[1]{0:T(128)S(6)} %copy.11.count_ref, bf16[1024,256]{1,0:T(8,128)(2,1)S(1)} %copy-done.2, ...), custom_call_target="tpu_custom_call" | custom-call | tf_op jit(solution)/shard_map/pairs/pallas_call | solution.py:179
  49.7 16.2 %all_to_all.11 = bf16[8,32,256]{2,1,0:T(8,128)(2,1)S(1)} all-to-all(bf16[8,32,256]{2,1,0:T(8,128)(2,1)S(1)} %bitcast.4), channel_id=1, replica_groups=mesh['chan'=64,'seg'=8] {'seg'}, dimensions={0} | all-to-all | bytes 262144 | tf_op jit(solution)/shard_map/all_to_all | solution.py:198
  65.9 0.6 convert_reduce_fusion
  (1 shorter events, 0.0 us)
Async XLA Ops:
  0.0 1.9 %copy-start = (bf16[4,1536,256]{2,1,0:T(8,128)(2,1)S(1)}, bf16[4,1536,256]{2,1,0:T(8,128)(2,1)}, u32[]{:S(2)}) copy-start(bf16[4,1536,256]{2,1,0:T(8,128)(2,1)} %constant.12.clone.table_hbm) | copy-start | bytes 9437188
  1.9 1.1 %copy-start.1 = (bf16[2,128,1536]{2,1,0:T(8,128)(2,1)S(1)}, bf16[2,128,1536]{2,1,0:T(8,128)(2,1)}, u32[]{:S(2)}) copy-start(bf16[2,128,1536]{2,1,0:T(8,128)(2,1)} %raw_hbm.1) | copy-start | bytes 2359300
  3.0 1.0 %copy-start.4 = (bf16[512,512]{1,0:T(8,128)(2,1)S(1)}, bf16[512,512]{1,0:T(8,128)(2,1)}, u32[]{:S(2)}) copy-start(bf16[512,512]{1,0:T(8,128)(2,1)} %constant.13.clone.band_hbm) | copy-start | bytes 1572868
  4.1 0.7 %copy-start.5 = (f32[1,512]{1,0:T(1,128)S(1)}, f32[1,512]{1,0:T(1,128)}, u32[]{:S(2)}) copy-start(f32[1,512]{1,0:T(1,128)} %constant.14.clone.inv_hbm) | copy-start | bytes 6148
  4.7 0.7 copy-start.8
  5.4 42.3 %copy-start.2 = (bf16[1024,256]{1,0:T(8,128)(2,1)S(1)}, bf16[1024,256]{1,0:T(8,128)(2,1)}, u32[]{:S(2)}) copy-start(bf16[1024,256]{1,0:T(8,128)(2,1)} %constant.15.clone.high_ref) | copy-start | bytes 1572868
  5.4 42.3 %copy-start.3 = (bf16[1024,256]{1,0:T(8,128)(2,1)S(1)}, bf16[1024,256]{1,0:T(8,128)(2,1)}, u32[]{:S(2)}) copy-start(bf16[1024,256]{1,0:T(8,128)(2,1)} %constant.16.clone.low_ref) | copy-start | bytes 1572868
  5.4 42.3 %copy-start.6 = (s32[256]{0:T(256)S(1)}, s32[256]{0:T(256)}, u32[]{:S(2)}) copy-start(s32[256]{0:T(256)} %param.12) | copy-start | bytes 3076
  5.4 42.3 %copy-start.7 = (s32[256]{0:T(256)S(1)}, s32[256]{0:T(256)}, u32[]{:S(2)}) copy-start(s32[256]{0:T(256)} %param.13) | copy-start | bytes 3076
  40.5 7.2 %collective-permute-start = (bf16[24,16,256]{2,1,0:T(8,128)(2,1)S(1)}, bf16[24,16,256]{2,1,0:T(8,128)(2,1)S(1)}, u32[]{:S(2)}, u32[]{:S(2)}) collective-permute-start(bf16[24,16,256]{2,1,0:T(8,128)(2,1)S(1)} %slice.4), channel_id=1, source_target_pairs={{8,0},{16,8},{24,16},{32,24},{40,32},{48,40},{56,48},{64,56},{72,6... | collective-permute-start | bytes 589832 | tf_op jit(solution)/shard_map/ppermute | solution.py:196

commit v2 on v1

--- a/solution.py
+++ b/solution.py
@@ -109,6 +109,10 @@
         out_ref[b * 16 : b * 16 + 16] = dot(mix, stacked).astype(BF).reshape(16, 16, COLS)
 
 
+def in_hbm(x):
+    return pltpu.with_memory_space_constraint(jnp.asarray(x), pltpu.HBM)
+
+
 def whitened(raw, send_order):
     near, inv = band_tables()
     hbm = pl.BlockSpec(memory_space=pltpu.HBM)
@@ -128,7 +132,7 @@
         ],
         compiler_params=pltpu.CompilerParams(vmem_limit_bytes=32 * 1024 * 1024),
         name="whiten",
-    )(raw, send_order.reshape(1, 128), forward_table(), near, inv)
+    )(*(in_hbm(x) for x in (raw, send_order.reshape(1, 128), forward_table(), near, inv)))
 
 
 def pairs_kernel(own_ref, rim_ref, first_ref, offset_ref, count_ref, high_ref, low_ref, out_ref, rows_ref):

time: 66.9 us -> 61.7 us (0.922)
  local copies, waits for them, and re-layouts: 5.43 us -> 0.03 us
    unnamed x18 -> x8, local copies, waits for them, and re-layouts: 5.41 us -> 0.02 us
where the time goes in v2:
time: 61.7 us; the launch traced here: 61.6 us
  blocking collectives  46.9 us (76%)
  Pallas kernels  6.76 us (11%)
  waiting for transfers between devices  3.48 us (6%)
  starting transfers between devices  3.07 us (5%)
  between operations  0.7 us (1%)
  other arithmetic  0.63 us (1%)
    all_to_all x1, blocking collectives, on_device(): own = lax.all_to_all(sent, 'chan', split_axis=0, concat_axis=0, tiled=True)  30.7 us
    all_to_all x1, blocking collectives, on_device(): lax.all_to_all(lags.reshape(groups, 256 // groups, LAGS), 'seg', 0, 0, ti...  16.2 us
    pallas_call x1, Pallas kernels, whitened(): pl.pallas_call(whiten_kernel, in_specs=[hbm] * 5, out_specs=pl.BlockSpec(...  4.79 us
    ppermute x1, waiting for transfers between devices, on_device(): lax.ppermute(own[:REACH // 2], 'chan', [(i + 1, i) for i in range(blocks...  3.48 us
    ppermute x1, starting transfers between devices, on_device(): lax.ppermute(own[:REACH // 2], 'chan', [(i + 1, i) for i in range(blocks...  3.07 us
    pallas_call x1, Pallas kernels, pair_lags(): pl.pallas_call(pairs_kernel, in_specs=[vmem, vmem, vmem, vmem, pl.BlockSp...  1.97 us
  transfers between devices with their start and end apart: 1, of which 1 were waited for; matrix products, arithmetic and copies ran while one was open for 0% of the time, Pallas kernels for 0%

profile of v2, /device:TPU:5, one launch (start us, length us, event | category | flops | bytes accessed | tf_op | source)
XLA Modules:
  0.0 61.6 jit_solution(15653599850051739428)
XLA Ops:
  0.0 0.0 copy-start
  0.0 0.0 copy-start.1
  0.0 0.0 copy-start.2
  0.0 0.0 copy-start.3
  0.0 4.8 %whiten.1 = bf16[64,16,256]{2,1,0:T(8,128)(2,1)S(1)} custom-call(bf16[2,128,1536]{2,1,0:T(8,128)(2,1)} %raw_hbm.1, s32[1,128]{1,0:T(1,128)} %bitcast.7, bf16[4,1536,256]{2,1,0:T(8,128)(2,1)} %constant.12.clone.table_hbm, bf16[512,512]{1,0:T(8,128)(2,1)} %constant.13.clone.band_hbm, f32[1,512]{1,0:T(1,128)} %constant.14.clone.inv_hbm), custom_call_target="tpu_custom_call" | custom-call | tf_op jit(solution)/shard_map/whiten/pallas_call | solution.py:119
  4.8 30.7 %all_to_all.10.own_ref = bf16[64,16,256]{2,1,0:T(8,128)(2,1)S(1)} all-to-all(bf16[64,16,256]{2,1,0:T(8,128)(2,1)S(1)} %whiten.1), channel_id=1, replica_groups=mesh['chan'=64,'seg'=8] {'chan'}, dimensions={0} | all-to-all | bytes 1048576 | tf_op jit(solution)/shard_map/all_to_all | solution.py:199
  35.6 3.1 %collective-permute-start = (bf16[24,16,256]{2,1,0:T(8,128)(2,1)S(1)}, bf16[24,16,256]{2,1,0:T(8,128)(2,1)S(1)}, u32[]{:S(2)}, u32[]{:S(2)}) collective-permute-start(bf16[24,16,256]{2,1,0:T(8,128)(2,1)S(1)} %slice.4), channel_id=1, source_target_pairs={{8,0},{16,8},{24,16},{32,24},{40,32},{48,40},{56,48},{64,56},{72,6... | collective-permute-start | bytes 589832 | tf_op jit(solution)/shard_map/ppermute | solution.py:200
  39.3 3.5 %collective-permute-done.rim_ref = bf16[24,16,256]{2,1,0:T(8,128)(2,1)S(1)} collective-permute-done((bf16[24,16,256]{2,1,0:T(8,128)(2,1)S(1)}, bf16[24,16,256]{2,1,0:T(8,128)(2,1)S(1)}, u32[]{:S(2)}, u32[]{:S(2)}) %collective-permute-start) | collective-permute-done | bytes 196640 | tf_op jit(solution)/shard_map/ppermute | solution.py:200
  42.8 0.0 copy-done
  42.8 0.0 copy-done.1
  42.8 0.0 copy-done.2
  42.8 0.0 copy-done.3
  42.8 2.0 %pairs.1 = bf16[256,256]{1,0:T(8,128)(2,1)S(1)} custom-call(bf16[64,16,256]{2,1,0:T(8,128)(2,1)S(1)} %all_to_all.10.own_ref, bf16[24,16,256]{2,1,0:T(8,128)(2,1)S(1)} %collective-permute-done.rim_ref, s32[1,256]{1,0:T(1,128)S(1)} %bitcast.5, s32[1,256]{1,0:T(1,128)S(1)} %bitcast.6, s32[1]{0:T(128)S(6)} %copy.11.count_ref, bf16[1024,256]{1,0:T(8,128)(2,1)S(1)} %copy-done, ...), custom_call_target="tpu_custom_call" | custom-call | tf_op jit(solution)/shard_map/pairs/pallas_call | solution.py:183
  44.8 16.2 %all_to_all.11 = bf16[8,32,256]{2,1,0:T(8,128)(2,1)S(1)} all-to-all(bf16[8,32,256]{2,1,0:T(8,128)(2,1)S(1)} %bitcast.4), channel_id=1, replica_groups=mesh['chan'=64,'seg'=8] {'seg'}, dimensions={0} | all-to-all | bytes 262144 | tf_op jit(solution)/shard_map/all_to_all | solution.py:202
  60.9 0.6 %convert_reduce_fusion = f32[32,256]{1,0:T(8,128)} fusion(bf16[8,32,256]{2,1,0:T(8,128)(2,1)S(1)} %all_to_all.11), kind=kLoop, calls=%fused_computation | loop fusion | flops 122880 | bytes 163840 | tf_op jit(solution)/shard_map/reduce_sum | solution.py:203
  (1 shorter events, 0.0 us)
Async XLA Ops:
  0.0 42.8 %copy-start = (bf16[1024,256]{1,0:T(8,128)(2,1)S(1)}, bf16[1024,256]{1,0:T(8,128)(2,1)}, u32[]{:S(2)}) copy-start(bf16[1024,256]{1,0:T(8,128)(2,1)} %constant.15.clone.high_ref) | copy-start | bytes 1572868
  0.0 42.8 %copy-start.1 = (bf16[1024,256]{1,0:T(8,128)(2,1)S(1)}, bf16[1024,256]{1,0:T(8,128)(2,1)}, u32[]{:S(2)}) copy-start(bf16[1024,256]{1,0:T(8,128)(2,1)} %constant.16.clone.low_ref) | copy-start | bytes 1572868
  0.0 42.8 %copy-start.2 = (s32[256]{0:T(256)S(1)}, s32[256]{0:T(256)}, u32[]{:S(2)}) copy-start(s32[256]{0:T(256)} %param.12) | copy-start | bytes 3076
  0.0 42.8 %copy-start.3 = (s32[256]{0:T(256)S(1)}, s32[256]{0:T(256)}, u32[]{:S(2)}) copy-start(s32[256]{0:T(256)} %param.13) | copy-start | bytes 3076
  35.6 7.2 %collective-permute-start = (bf16[24,16,256]{2,1,0:T(8,128)(2,1)S(1)}, bf16[24,16,256]{2,1,0:T(8,128)(2,1)S(1)}, u32[]{:S(2)}, u32[]{:S(2)}) collective-permute-start(bf16[24,16,256]{2,1,0:T(8,128)(2,1)S(1)} %slice.4), channel_id=1, source_target_pairs={{8,0},{16,8},{24,16},{32,24},{40,32},{48,40},{56,48},{64,56},{72,6... | collective-permute-start | bytes 589832 | tf_op jit(solution)/shard_map/ppermute | solution.py:200

commit v3 on v2

--- a/solution.py
+++ b/solution.py
@@ -19,23 +19,19 @@
 F32 = jnp.float32
 
 
+BINS = (1 + np.arange(STEPS)[:, None] + STEPS * np.arange(F // STEPS)[None, :]).reshape(F)
+
+
 def forward_table():
-    bins = 1 + np.arange(F)
-    samples = np.arange(L)
-    phase = (samples[:, None] * bins[None, :] % L).astype(np.float32) * np.float32(2.0 * math.pi / L)
-    cosines = np.cos(phase).astype(BF).reshape(L, STEPS, F // STEPS)
-    sines = (-np.sin(phase)).astype(BF).reshape(L, STEPS, F // STEPS)
+    quarter = L // 4
+    phase = (np.arange(quarter)[:, None] * BINS[None, :] % L).astype(np.float32) * np.float32(2.0 * math.pi / L)
+    cosines = np.cos(phase).astype(BF).reshape(quarter, STEPS, F // STEPS)
+    sines = (-np.sin(phase)).astype(BF).reshape(quarter, STEPS, F // STEPS)
     return np.ascontiguousarray(np.concatenate([cosines, sines], axis=-1).transpose(1, 0, 2))
 
 
-def band_tables():
-    bin_index = np.arange(F)
-    nearby = np.abs(bin_index[:, None] - bin_index[None, :]) <= BAND
-    return nearby.astype(BF), (1.0 / nearby.sum(axis=0, keepdims=True)).astype(np.float32)
-
-
 def inverse_tables(factor):
-    bins = 1 + np.arange(F)
+    bins = BINS
     lag_shift = np.arange(LAGS) - LAGS // 2
     phase = (bins[:, None] * lag_shift[None, :] % L).astype(np.float64) * (2.0 * math.pi / L)
     table = (np.concatenate([np.cos(phase), -np.sin(phase)], axis=0) * factor).astype(np.float32)
@@ -49,52 +45,86 @@
 
 def spread_matrix(blocks, back):
     rows = blocks * 16
-    r = lax.broadcasted_iota(jnp.int32, (rows, rows), 0)
-    k = lax.broadcasted_iota(jnp.int32, (rows, rows), 1)
-    mixed, apart = (k, r) if back else (r, k)
-    p, cs, j = mixed // 16, (mixed % 16) // 2, mixed % 2
-    return (apart == cs * (2 * blocks) + p * 2 + j).astype(F32).astype(BF)
-
-
-def whiten_kernel(
-    raw_hbm, order_hbm, table_hbm, band_hbm, inv_hbm, out_ref, raw_ref, order_ref, table_ref, band_ref, inv_ref, normed, sems
-):
+    shape = (1, rows) if back else (rows, 1)
+    mixed = lax.broadcasted_iota(jnp.int32, shape, 1 if back else 0)
+    target = (mixed % 16) // 2 * (2 * blocks) + mixed // 16 * 2 + mixed % 2
+    apart = lax.broadcasted_iota(jnp.int32, (rows, rows), 0 if back else 1)
+    return (apart == target).astype(F32).astype(BF)
+
+
+def split(x):
+    high = x.astype(BF)
+    return high, (x - high.astype(F32)).astype(BF)
+
+
+def fold(normed, even, odd, first_row):
+    quarter = L // 4
+    x0, x1, x2, x3 = (normed[:, i * quarter : (i + 1) * quarter] for i in range(4))
+    even0, even1 = x0 + x2, x1 + x3
+    count = normed.shape[0]
+    upper, lower = slice(first_row, first_row + count), slice(first_row + 256, first_row + 256 + count)
+    for at, value in enumerate((even0 - even1, even0 + even1)):
+        even[at, upper], even[at, lower] = split(value)
+    for side, value in enumerate((x0 - x2, x1 - x3)):
+        columns = slice(side * quarter, (side + 1) * quarter)
+        odd[upper, columns], odd[lower, columns] = split(value)
+
+
+def whiten_kernel(raw_hbm, order_hbm, table_hbm, out_ref, raw_ref, order_ref, table_ref, even, odd, sems):
     width = F // STEPS
     half = F // 2
-    copies = [pltpu.make_async_copy(raw_hbm.at[s], raw_ref.at[s], sems.at[s]) for s in range(2)]
-    copies += [pltpu.make_async_copy(table_hbm.at[i], table_ref.at[i], sems.at[2 + i]) for i in range(STEPS)]
-    copies += [
-        pltpu.make_async_copy(band_hbm, band_ref, sems.at[2 + STEPS]),
-        pltpu.make_async_copy(inv_hbm, inv_ref, sems.at[3 + STEPS]),
-        pltpu.make_async_copy(order_hbm, order_ref, sems.at[4 + STEPS]),
-    ]
-    for copy in copies:
+    quarter = L // 4
+    visit = (0, 2, 1, 3)
+    raw_copies = [pltpu.make_async_copy(raw_hbm.at[s], raw_ref.at[s], sems.at[s]) for s in range(2)]
+    table_copies = {
+        i: pltpu.make_async_copy(table_hbm.at[i], table_ref.at[i, :quarter], sems.at[2 + i]) for i in visit
+    }
+    order_copy = pltpu.make_async_copy(order_hbm, order_ref, sems.at[2 + STEPS])
+    for copy in (*raw_copies, *table_copies.values(), order_copy):
         copy.start()
     mix = spread_matrix(16, False)
+
+    def bin_at(position):
+        return (position % width) * STEPS + position // width + 1
+
+    bin_row = bin_at(lax.broadcasted_iota(jnp.int32, (F, 1), 0))
+    bin_line = bin_at(lax.broadcasted_iota(jnp.int32, (1, F), 1))
+    near = (jnp.abs(bin_row - bin_line) <= BAND).astype(F32).astype(BF)
+    count = jnp.minimum(bin_line + BAND, F) - jnp.maximum(bin_line - BAND, 1) + 1
+    share = 1.0 / count.astype(F32)
+
     for s in range(2):
-        copies[s].wait()
-        wave = raw_ref[s].astype(F32)
-        mean = jnp.sum(wave * wave, axis=-1, keepdims=True) * (1.0 / L)
-        normed[s * 128 : s * 128 + 128] = (wave * lax.rsqrt(mean + 1e-05)).astype(BF)
-    real, imag = [], []
+        raw_copies[s].wait()
+        for r in range(0, 128, 32):
+            wave = raw_ref[s, r : r + 32].astype(F32)
+            mean = jnp.sum(wave * wave, axis=-1, keepdims=True) * (1.0 / L)
+            normed = (wave * lax.rsqrt(mean + 1e-05)).astype(BF).astype(F32)
+            fold(normed, even, odd, s * 128 + r)
+    for i in (0, 2):
+        table_copies[i].wait()
+        cosines = table_ref[i, :quarter, :width]
+        sines = table_ref[i, :quarter, width:]
+        table_ref[i, quarter:, :width] = sines if i == 0 else -sines
+        table_ref[i, quarter:, width:] = -cosines if i == 0 else cosines
+    real, imag = {}, {}
     smooth = None
-    for i in range(STEPS):
-        copies[2 + i].wait()
-        spec = dot(normed[...], table_ref[i])
-        real.append(spec[:, :width])
-        imag.append(spec[:, width:])
-        if i == 1:
-            copies[2 + STEPS].wait()
+    for i in visit:
         if i % 2:
-            power = jnp.concatenate([real[k] * real[k] + imag[k] * imag[k] for k in (i - 1, i)], axis=1)
-            high = power.astype(BF)
-            low = (power - high.astype(F32)).astype(BF)
-            near = band_ref[(i // 2) * half : (i // 2 + 1) * half]
-            part = dot(high, near) + dot(low, near)
-            smooth = part if smooth is None else smooth + part
-    for copy in copies[3 + STEPS :]:
-        copy.wait()
-    factor = lax.rsqrt(smooth * inv_ref[...] + 1e-06)
+            table_copies[i].wait()
+            both = dot(even[i // 2], table_ref[i, :quarter])
+        else:
+            both = dot(odd[...], table_ref[i])
+        spec = both[:256] + both[256:]
+        real[i] = spec[:, :width]
+        imag[i] = spec[:, width:]
+    for pair in ((0, 1), (2, 3)):
+        power = jnp.concatenate([real[k] * real[k] + imag[k] * imag[k] for k in pair], axis=1)
+        high, low = split(power)
+        rows = near[pair[0] * width : pair[0] * width + half]
+        part = dot(high, rows) + dot(low, rows)
+        smooth = part if smooth is None else smooth + part
+    order_copy.wait()
+    factor = lax.rsqrt(smooth * share + 1e-06)
     channels = lax.broadcasted_iota(jnp.int32, (128, 128), 0)
     pick = (channels == order_ref[...]).astype(F32).T.astype(BF)
     picked = []
@@ -114,25 +144,23 @@
 
 
 def whitened(raw, send_order):
-    near, inv = band_tables()
     hbm = pl.BlockSpec(memory_space=pltpu.HBM)
     return pl.pallas_call(
         whiten_kernel,
-        in_specs=[hbm] * 5,
+        in_specs=[hbm] * 3,
         out_specs=pl.BlockSpec(memory_space=pltpu.VMEM),
         out_shape=jax.ShapeDtypeStruct((64, 16, COLS), BF),
         scratch_shapes=[
             pltpu.VMEM((2, 128, L), BF),
             pltpu.VMEM((1, 128), jnp.int32),
-            pltpu.VMEM((STEPS, L, COLS), BF),
-            pltpu.VMEM((F, F), BF),
-            pltpu.VMEM((1, F), F32),
-            pltpu.VMEM((256, L), BF),
-            pltpu.SemaphoreType.DMA((5 + STEPS,)),
+            pltpu.VMEM((STEPS, L // 2, COLS), BF),
+            pltpu.VMEM((2, 512, L // 4), BF),
+            pltpu.VMEM((512, L // 2), BF),
+            pltpu.SemaphoreType.DMA((3 + STEPS,)),
         ],
         compiler_params=pltpu.CompilerParams(vmem_limit_bytes=32 * 1024 * 1024),
         name="whiten",
-    )(*(in_hbm(x) for x in (raw, send_order.reshape(1, 128), forward_table(), near, inv)))
+    )(*(in_hbm(x) for x in (raw, send_order.reshape(1, 128), forward_table())))
 
 
 def pairs_kernel(own_ref, rim_ref, first_ref, offset_ref, count_ref, high_ref, low_ref, out_ref, rows_ref):

time: 61.7 us -> 62 us (level)
  local copies, waits for them, and re-layouts: 0.03 us -> 0.7 us
  Pallas kernels: 6.76 us -> 6.11 us
    unnamed x8, local copies, waits for them, and re-layouts: 0.02 us -> 0.69 us
    pallas_call x1, Pallas kernels: 4.79 us -> 4.15 us  [whitened(): pl.pallas_call(whiten_kernel, in_specs=[hbm] * 3, out_specs=pl.BlockSpec(...]
where the time goes in v3:
time: 62 us; the launch traced here: 61.7 us
  blocking collectives  47 us (76%)
  Pallas kernels  6.11 us (10%)
  waiting for transfers between devices  3.48 us (6%)
  starting transfers between devices  3.07 us (5%)
  local copies, waits for them, and re-layouts  0.7 us (1%)
  between operations  0.7 us (1%)
  other arithmetic  0.63 us (1%)
    all_to_all x1, blocking collectives, on_device(): own = lax.all_to_all(sent, 'chan', split_axis=0, concat_axis=0, tiled=True)  30.9 us
    all_to_all x1, blocking collectives, on_device(): lax.all_to_all(lags.reshape(groups, 256 // groups, LAGS), 'seg', 0, 0, ti...  16.2 us
    pallas_call x1, Pallas kernels, whitened(): pl.pallas_call(whiten_kernel, in_specs=[hbm] * 3, out_specs=pl.BlockSpec(...  4.15 us
    ppermute x1, waiting for transfers between devices, on_device(): lax.ppermute(own[:REACH // 2], 'chan', [(i + 1, i) for i in range(blocks...  3.48 us
    ppermute x1, starting transfers between devices, on_device(): lax.ppermute(own[:REACH // 2], 'chan', [(i + 1, i) for i in range(blocks...  3.07 us
    pallas_call x1, Pallas kernels, pair_lags(): pl.pallas_call(pairs_kernel, in_specs=[vmem, vmem, vmem, vmem, pl.BlockSp...  1.97 us
  transfers between devices with their start and end apart: 1, of which 1 were waited for; matrix products, arithmetic and copies ran while one was open for 0% of the time, Pallas kernels for 0%

profile of v3, /device:TPU:5, one launch (start us, length us, event | category | flops | bytes accessed | tf_op | source)
XLA Modules:
  0.0 61.7 jit_solution(15616685827226895455)
XLA Ops:
  0.0 4.1 %whiten.1 = bf16[64,16,256]{2,1,0:T(8,128)(2,1)S(1)} custom-call(bf16[2,128,1536]{2,1,0:T(8,128)(2,1)} %raw_hbm.1, s32[1,128]{1,0:T(1,128)} %bitcast.7, bf16[4,384,256]{2,1,0:T(8,128)(2,1)} %constant.8.clone.table_hbm), custom_call_target="tpu_custom_call" | custom-call | tf_op jit(solution)/shard_map/whiten/pallas_call | solution.py:148
  4.2 0.0 copy-start
  4.2 0.0 copy-start.1
  4.2 30.9 %all_to_all.10.own_ref = bf16[64,16,256]{2,1,0:T(8,128)(2,1)S(1)} all-to-all(bf16[64,16,256]{2,1,0:T(8,128)(2,1)S(1)} %whiten.1), channel_id=1, replica_groups=mesh['chan'=64,'seg'=8] {'chan'}, dimensions={0} | all-to-all | bytes 1048576 | tf_op jit(solution)/shard_map/all_to_all | solution.py:227
  35.0 0.0 copy-start.3
  35.1 3.1 %collective-permute-start = (bf16[24,16,256]{2,1,0:T(8,128)(2,1)S(1)}, bf16[24,16,256]{2,1,0:T(8,128)(2,1)S(1)}, u32[]{:S(2)}, u32[]{:S(2)}) collective-permute-start(bf16[24,16,256]{2,1,0:T(8,128)(2,1)S(1)} %slice.4), channel_id=1, source_target_pairs={{8,0},{16,8},{24,16},{32,24},{40,32},{48,40},{56,48},{64,56},{72,6... | collective-permute-start | bytes 589832 | tf_op jit(solution)/shard_map/ppermute | solution.py:228
  38.8 3.5 %collective-permute-done.rim_ref = bf16[24,16,256]{2,1,0:T(8,128)(2,1)S(1)} collective-permute-done((bf16[24,16,256]{2,1,0:T(8,128)(2,1)S(1)}, bf16[24,16,256]{2,1,0:T(8,128)(2,1)S(1)}, u32[]{:S(2)}, u32[]{:S(2)}) %collective-permute-start) | collective-permute-done | bytes 196640 | tf_op jit(solution)/shard_map/ppermute | solution.py:228
  42.3 0.0 copy-start.2
  42.3 0.0 copy-done
  42.3 0.0 copy-done.1
  42.3 0.0 copy-done.3
  42.3 0.7 %copy-done.2 = s32[256]{0:T(256)S(1)} copy-done((s32[256]{0:T(256)S(1)}, s32[256]{0:T(256)}, u32[]{:S(2)}) %copy-start.2) | copy-done | bytes 1048
  42.9 2.0 %pairs.1 = bf16[256,256]{1,0:T(8,128)(2,1)S(1)} custom-call(bf16[64,16,256]{2,1,0:T(8,128)(2,1)S(1)} %all_to_all.10.own_ref, bf16[24,16,256]{2,1,0:T(8,128)(2,1)S(1)} %collective-permute-done.rim_ref, s32[1,256]{1,0:T(1,128)S(1)} %bitcast.5, s32[1,256]{1,0:T(1,128)S(1)} %bitcast.6, s32[1]{0:T(128)S(6)} %copy.9.count_ref, bf16[1024,256]{1,0:T(8,128)(2,1)S(1)} %copy-done.1, ...), custom_call_target="tpu_custom_call" | custom-call | tf_op jit(solution)/shard_map/pairs/pallas_call | solution.py:211
  44.9 16.2 %all_to_all.11 = bf16[8,32,256]{2,1,0:T(8,128)(2,1)S(1)} all-to-all(bf16[8,32,256]{2,1,0:T(8,128)(2,1)S(1)} %bitcast.4), channel_id=1, replica_groups=mesh['chan'=64,'seg'=8] {'seg'}, dimensions={0} | all-to-all | bytes 262144 | tf_op jit(solution)/shard_map/all_to_all | solution.py:230
  61.1 0.6 %convert_reduce_fusion = f32[32,256]{1,0:T(8,128)} fusion(bf16[8,32,256]{2,1,0:T(8,128)(2,1)S(1)} %all_to_all.11), kind=kLoop, calls=%fused_computation | loop fusion | flops 122880 | bytes 163840 | tf_op jit(solution)/shard_map/reduce_sum | solution.py:231
  (1 shorter events, 0.0 us)
Async XLA Ops:
  4.2 38.1 %copy-start = (bf16[1024,256]{1,0:T(8,128)(2,1)S(1)}, bf16[1024,256]{1,0:T(8,128)(2,1)}, u32[]{:S(2)}) copy-start(bf16[1024,256]{1,0:T(8,128)(2,1)} %constant.10.clone.low_ref) | copy-start | bytes 1572868
  4.2 38.1 %copy-start.1 = (bf16[1024,256]{1,0:T(8,128)(2,1)S(1)}, bf16[1024,256]{1,0:T(8,128)(2,1)}, u32[]{:S(2)}) copy-start(bf16[1024,256]{1,0:T(8,128)(2,1)} %constant.9.clone.high_ref) | copy-start | bytes 1572868
  35.0 7.2 %copy-start.3 = (s32[256]{0:T(256)S(1)}, s32[256]{0:T(256)}, u32[]{:S(2)}) copy-start(s32[256]{0:T(256)} %param.11) | copy-start | bytes 3076
  35.1 7.2 %collective-permute-start = (bf16[24,16,256]{2,1,0:T(8,128)(2,1)S(1)}, bf16[24,16,256]{2,1,0:T(8,128)(2,1)S(1)}, u32[]{:S(2)}, u32[]{:S(2)}) collective-permute-start(bf16[24,16,256]{2,1,0:T(8,128)(2,1)S(1)} %slice.4), channel_id=1, source_target_pairs={{8,0},{16,8},{24,16},{32,24},{40,32},{48,40},{56,48},{64,56},{72,6... | collective-permute-start | bytes 589832 | tf_op jit(solution)/shard_map/ppermute | solution.py:228
  42.3 0.7 %copy-start.2 = (s32[256]{0:T(256)S(1)}, s32[256]{0:T(256)}, u32[]{:S(2)}) copy-start(s32[256]{0:T(256)} %param.10) | copy-start | bytes 3076

commit v4 on v3

--- a/solution.py
+++ b/solution.py
@@ -163,7 +163,15 @@
     )(*(in_hbm(x) for x in (raw, send_order.reshape(1, 128), forward_table())))
 
 
-def pairs_kernel(own_ref, rim_ref, first_ref, offset_ref, count_ref, high_ref, low_ref, out_ref, rows_ref):
+def gather_kernel(
+    own_ref, count_ref, first_hbm, offset_hbm, high_hbm, low_hbm,
+    left_ref, right_ref, pick_ref, high_ref, low_ref,
+    rows_ref, first_ref, offset_ref, sems,
+):
+    moves = ((first_hbm, first_ref), (offset_hbm, offset_ref), (high_hbm, high_ref), (low_hbm, low_ref))
+    copies = [pltpu.make_async_copy(src, dst, sems.at[i]) for i, (src, dst) in enumerate(moves)]
+    for copy in copies:
+        copy.start()
     apart = spread_matrix(16, True)
     for b in range(4):
         block = dot(apart, own_ref[b * 16 : b * 16 + 16].reshape(256, COLS)).astype(BF)
@@ -171,52 +179,84 @@
             for s in range(2):
                 at = (c * 2 + s) * 32
                 rows_ref[s, c, b * 32 : b * 32 + 32] = block[at : at + 32]
-    apart = spread_matrix(8, True)
-    for b in range(3):
-        block = dot(apart, rim_ref[b * 8 : b * 8 + 8].reshape(128, COLS)).astype(BF)
-        for c in range(4):
-            for s in range(2):
-                at = (c * 2 + s) * 16
-                rows_ref[s, c, 128 + b * 16 : 128 + b * 16 + 16] = block[at : at + 16]
+    for copy in copies[:2]:
+        copy.wait()
     first = first_ref[...]
     second = first + offset_ref[...]
     slot = lax.broadcasted_iota(jnp.int32, (1, 256), 1)
-    first = jnp.where(slot < count_ref[0], first, -1)
-    left_at = lax.broadcasted_iota(jnp.int32, (128, 256), 0)
-    left_pick = (left_at == first).astype(F32).T.astype(BF)
-    right_at = lax.broadcasted_iota(jnp.int32, (176, 256), 0)
-    right_pick = (right_at == second).astype(F32).T.astype(BF)
-    total = jnp.zeros((256, LAGS), F32)
+    live_first = jnp.where(slot < count_ref[0], first, -1)
+    at = lax.broadcasted_iota(jnp.int32, (128, 256), 0)
+    left_pick = (at == live_first).astype(F32).T.astype(BF)
+    right_pick = (at == second).astype(F32).T.astype(BF)
+    pick_ref[...] = (at + 128 == second).astype(F32).T.astype(BF)
+    for s in range(2):
+        for c in range(4):
+            rows = rows_ref[s, c]
+            left_ref[s, c] = dot(left_pick, rows).astype(BF)
+            right_ref[s, c] = dot(right_pick, rows).astype(BF)
+    for copy in copies[2:]:
+        copy.wait()
+
+
+def gathered(own, pair_first, pair_offset, pair_count, factor):
+    high, low = inverse_tables(factor)
+    vmem = pl.BlockSpec(memory_space=pltpu.VMEM)
+    hbm = pl.BlockSpec(memory_space=pltpu.HBM)
+    rows = jax.ShapeDtypeStruct((2, 4, 256, COLS), BF)
+    table = jax.ShapeDtypeStruct((2 * F, LAGS), BF)
+    return pl.pallas_call(
+        gather_kernel,
+        in_specs=[vmem, pl.BlockSpec(memory_space=pltpu.SMEM)] + [hbm] * 4,
+        out_specs=[vmem] * 5,
+        out_shape=[rows, rows, jax.ShapeDtypeStruct((256, 128), BF), table, table],
+        scratch_shapes=[
+            pltpu.VMEM((2, 4, 128, COLS), BF),
+            pltpu.VMEM((1, 256), jnp.int32),
+            pltpu.VMEM((1, 256), jnp.int32),
+            pltpu.SemaphoreType.DMA((4,)),
+        ],
+        compiler_params=pltpu.CompilerParams(vmem_limit_bytes=32 * 1024 * 1024),
+        name="gather",
+    )(own, pair_count, *(in_hbm(x) for x in (pair_first.reshape(1, 256), pair_offset.reshape(1, 256), high, low)))
+
+
+def pairs_kernel(rim_ref, left_ref, right_ref, pick_ref, high_ref, low_ref, out_ref):
+    apart = spread_matrix(8, True)
+    blocks = [dot(apart, rim_ref[b * 8 : b * 8 + 8].reshape(128, COLS)).astype(BF) for b in range(3)]
+    pick = pick_ref[:, :REACH]
+
+    def right(s, c):
+        at = (c * 2 + s) * 16
+        rim_rows = jnp.concatenate([block[at : at + 16] for block in blocks], axis=0)
+        return right_ref[s, c].astype(F32) + dot(pick, rim_rows)
+
+    highs, lows = {}, {}
     for c in range(2):
-        re = jnp.zeros((256, COLS), F32)
-        im = jnp.zeros((256, COLS), F32)
+        re = im = None
         for s in range(2):
-            a_re = dot(left_pick, rows_ref[s, c, :128])
-            a_im = dot(left_pick, rows_ref[s, c + 2, :128])
-            c_re = dot(right_pick, rows_ref[s, c])
-            c_im = dot(right_pick, rows_ref[s, c + 2])
-            re += a_re * c_re + a_im * c_im
-            im += a_im * c_re - a_re * c_im
-        for part, row in ((re, c * COLS), (im, (c + 2) * COLS)):
-            high = part.astype(BF)
-            low = (part - high.astype(F32)).astype(BF)
-            table = high_ref[row : row + COLS]
-            total += dot(high, table) + dot(low, table) + dot(high, low_ref[row : row + COLS])
+            a_re, a_im = left_ref[s, c].astype(F32), left_ref[s, c + 2].astype(F32)
+            c_re, c_im = right(s, c), right(s, c + 2)
+            one, two = a_re * c_re + a_im * c_im, a_im * c_re - a_re * c_im
+            re = one if re is None else re + one
+            im = two if im is None else im + two
+        highs[c], lows[c] = split(re)
+        highs[c + 2], lows[c + 2] = split(im)
+    high = jnp.concatenate([highs[c] for c in range(4)], axis=1)
+    low = jnp.concatenate([lows[c] for c in range(4)], axis=1)
+    total = dot(high, high_ref[...]) + dot(low, high_ref[...]) + dot(high, low_ref[...])
     out_ref[...] = total.astype(BF)
 
 
-def pair_lags(own, rim, pair_first, pair_offset, pair_count, factor):
-    high, low = inverse_tables(factor)
+def pair_lags(rim, parts):
     vmem = pl.BlockSpec(memory_space=pltpu.VMEM)
     return pl.pallas_call(
         pairs_kernel,
-        in_specs=[vmem, vmem, vmem, vmem, pl.BlockSpec(memory_space=pltpu.SMEM), vmem, vmem],
+        in_specs=[vmem] * 6,
         out_specs=vmem,
         out_shape=jax.ShapeDtypeStruct((256, LAGS), BF),
-        scratch_shapes=[pltpu.VMEM((2, 4, 176, COLS), BF)],
         compiler_params=pltpu.CompilerParams(vmem_limit_bytes=32 * 1024 * 1024),
         name="pairs",
-    )(own, rim, pair_first.reshape(1, 256), pair_offset.reshape(1, 256), pair_count, high, low)
+    )(rim, *parts)
 
 
 def on_device(raw, send_order, pair_first, pair_offset, pair_count):
@@ -226,7 +266,8 @@
     sent = whitened(raw, send_order)
     own = lax.all_to_all(sent, "chan", split_axis=0, concat_axis=0, tiled=True)
     rim = lax.ppermute(own[: REACH // 2], "chan", [(i + 1, i) for i in range(blocks - 1)])
-    lags = pair_lags(own, rim, pair_first, pair_offset, pair_count, 1.0 / math.sqrt(seg_count * groups * F))
+    parts = gathered(own, pair_first, pair_offset, pair_count, 1.0 / math.sqrt(seg_count * groups * F))
+    lags = pair_lags(rim, parts)
     shares = lax.all_to_all(lags.reshape(groups, 256 // groups, LAGS), "seg", 0, 0, tiled=True)
     return jnp.sum(shares.astype(F32), axis=0)
 

time: 62 us -> 61 us (0.984)
  waiting for transfers between devices: 3.48 us -> 1.91 us
  Pallas kernels: 6.11 us -> 7.55 us
  local copies, waits for them, and re-layouts: 0.7 us -> 0.01 us
    ppermute x1, waiting for transfers between devices: 3.48 us -> 1.91 us  [on_device(): lax.ppermute(own[:REACH // 2], 'chan', [(i + 1, i) for i in range(blocks...]
    pallas_call x1 -> x2, Pallas kernels: 1.97 us -> 3.4 us  [the longest x1 1.84 us: pair_lags(): pl.pallas_call(pairs_kernel, in_specs=[vmem] * 6, out_specs=vmem, out_sha...]
    unnamed x8 -> x0, local copies, waits for them, and re-layouts: 0.69 us -> none
  transfers between devices with their start and end apart: 1 -> 1, of which waited for: 1 -> 1; matrix products, arithmetic and copies ran while one was open for 0% -> 0% of each run, Pallas kernels for 0% -> 3%
where the time goes in v4:
time: 61 us; the launch traced here: 60.8 us
  blocking collectives  46.9 us (77%)
  Pallas kernels  7.55 us (12%)
  starting transfers between devices  3.07 us (5%)
  waiting for transfers between devices  1.91 us (3%)
  between operations  0.68 us (1%)
  other arithmetic  0.63 us (1%)
    all_to_all x1, blocking collectives, on_device(): own = lax.all_to_all(sent, 'chan', split_axis=0, concat_axis=0, tiled=True)  30.7 us
    all_to_all x1, blocking collectives, on_device(): lax.all_to_all(lags.reshape(groups, 256 // groups, LAGS), 'seg', 0, 0, ti...  16.2 us
    pallas_call x1, Pallas kernels, whitened(): pl.pallas_call(whiten_kernel, in_specs=[hbm] * 3, out_specs=pl.BlockSpec(...  4.15 us
    ppermute x1, starting transfers between devices, on_device(): lax.ppermute(own[:REACH // 2], 'chan', [(i + 1, i) for i in range(blocks...  3.07 us
    ppermute x1, waiting for transfers between devices, on_device(): lax.ppermute(own[:REACH // 2], 'chan', [(i + 1, i) for i in range(blocks...  1.91 us
    pallas_call x1, Pallas kernels, pair_lags(): pl.pallas_call(pairs_kernel, in_specs=[vmem] * 6, out_specs=vmem, out_sha...  1.84 us
    pallas_call x1, Pallas kernels, gathered(): pl.pallas_call(gather_kernel, in_specs=[vmem, pl.BlockSpec(memory_space=p...  1.57 us
  transfers between devices with their start and end apart: 1, of which 1 were waited for; matrix products, arithmetic and copies ran while one was open for 0% of the time, Pallas kernels for 3%

profile of v4, /device:TPU:5, one launch (start us, length us, event | category | flops | bytes accessed | tf_op | source)
XLA Modules:
  0.0 60.8 jit_solution(16705462499592476192)
XLA Ops:
  0.0 4.1 %whiten.1 = bf16[64,16,256]{2,1,0:T(8,128)(2,1)S(1)} custom-call(bf16[2,128,1536]{2,1,0:T(8,128)(2,1)} %raw_hbm.1, s32[1,128]{1,0:T(1,128)} %bitcast.7, bf16[4,384,256]{2,1,0:T(8,128)(2,1)} %constant.8.clone.table_hbm), custom_call_target="tpu_custom_call" | custom-call | tf_op jit(solution)/shard_map/whiten/pallas_call | solution.py:148
  4.2 30.7 %all_to_all.10.own_ref = bf16[64,16,256]{2,1,0:T(8,128)(2,1)S(1)} all-to-all(bf16[64,16,256]{2,1,0:T(8,128)(2,1)S(1)} %whiten.1), channel_id=1, replica_groups=mesh['chan'=64,'seg'=8] {'chan'}, dimensions={0} | all-to-all | bytes 1048576 | tf_op jit(solution)/shard_map/all_to_all | solution.py:267
  34.9 3.1 %collective-permute-start = (bf16[24,16,256]{2,1,0:T(8,128)(2,1)S(1)}, bf16[24,16,256]{2,1,0:T(8,128)(2,1)S(1)}, u32[]{:S(2)}, u32[]{:S(2)}) collective-permute-start(bf16[24,16,256]{2,1,0:T(8,128)(2,1)S(1)} %slice.4), channel_id=1, source_target_pairs={{8,0},{16,8},{24,16},{32,24},{40,32},{48,40},{56,48},{64,56},{72,6... | collective-permute-start | bytes 589832 | tf_op jit(solution)/shard_map/ppermute | solution.py:268
  38.6 1.6 %gather.1 = (bf16[2,4,256,256]{3,2,1,0:T(8,128)(2,1)S(1)}, bf16[2,4,256,256]{3,2,1,0:T(8,128)(2,1)S(1)}, bf16[256,128]{1,0:T(8,128)(2,1)S(1)}, bf16[1024,256]{1,0:T(8,128)(2,1)S(1)}, bf16[1024,256]{1,0:T(8,128)(2,1)S(1)}) custom-call(bf16[64,16,256]{2,1,0:T(8,128)(2,1)S(1)} %all_to_all.10.own_ref, s32[1]{0:T(128)S(6)} %copy.9.count_ref, s32[1,256]{1,0:T(1,128)} %bitcast.5, ...), custom_call_target="tpu_custom_call" | custom-call | tf_op jit(solution)/shard_map/gather/pallas_call | solution.py:207
  40.2 1.9 %collective-permute-done.rim_ref = bf16[24,16,256]{2,1,0:T(8,128)(2,1)S(1)} collective-permute-done((bf16[24,16,256]{2,1,0:T(8,128)(2,1)S(1)}, bf16[24,16,256]{2,1,0:T(8,128)(2,1)S(1)}, u32[]{:S(2)}, u32[]{:S(2)}) %collective-permute-start) | collective-permute-done | bytes 196640 | tf_op jit(solution)/shard_map/ppermute | solution.py:268
  42.1 1.8 %pairs.1 = bf16[256,256]{1,0:T(8,128)(2,1)S(1)} custom-call(bf16[24,16,256]{2,1,0:T(8,128)(2,1)S(1)} %collective-permute-done.rim_ref, bf16[2,4,256,256]{3,2,1,0:T(8,128)(2,1)S(1)} %get-tuple-element.10.left_ref, bf16[2,4,256,256]{3,2,1,0:T(8,128)(2,1)S(1)} %get-tuple-element.11.right_ref, bf16[256,128]{1,0:T(8,128)(2,1)S(1)} %get-tuple-element.12.pick_ref, ...), custom_call_target="tpu_custom_call" | custom-call | tf_op jit(solution)/shard_map/pairs/pallas_call | solution.py:252
  43.9 16.2 %all_to_all.11 = bf16[8,32,256]{2,1,0:T(8,128)(2,1)S(1)} all-to-all(bf16[8,32,256]{2,1,0:T(8,128)(2,1)S(1)} %bitcast.4), channel_id=1, replica_groups=mesh['chan'=64,'seg'=8] {'seg'}, dimensions={0} | all-to-all | bytes 262144 | tf_op jit(solution)/shard_map/all_to_all | solution.py:271
  60.1 0.6 %convert_reduce_fusion = f32[32,256]{1,0:T(8,128)} fusion(bf16[8,32,256]{2,1,0:T(8,128)(2,1)S(1)} %all_to_all.11), kind=kLoop, calls=%fused_computation | loop fusion | flops 122880 | bytes 163840 | tf_op jit(solution)/shard_map/reduce_sum | solution.py:272
  (1 shorter events, 0.0 us)
Async XLA Ops:
  34.9 7.2 %collective-permute-start = (bf16[24,16,256]{2,1,0:T(8,128)(2,1)S(1)}, bf16[24,16,256]{2,1,0:T(8,128)(2,1)S(1)}, u32[]{:S(2)}, u32[]{:S(2)}) collective-permute-start(bf16[24,16,256]{2,1,0:T(8,128)(2,1)S(1)} %slice.4), channel_id=1, source_target_pairs={{8,0},{16,8},{24,16},{32,24},{40,32},{48,40},{56,48},{64,56},{72,6... | collective-permute-start | bytes 589832 | tf_op jit(solution)/shard_map/ppermute | solution.py:268

commit v5 on v4

--- a/solution.py
+++ b/solution.py
@@ -72,7 +72,6 @@
 
 def whiten_kernel(raw_hbm, order_hbm, table_hbm, out_ref, raw_ref, order_ref, table_ref, even, odd, sems):
     width = F // STEPS
-    half = F // 2
     quarter = L // 4
     visit = (0, 2, 1, 3)
     raw_copies = [pltpu.make_async_copy(raw_hbm.at[s], raw_ref.at[s], sems.at[s]) for s in range(2)]
@@ -107,7 +106,6 @@
         table_ref[i, quarter:, :width] = sines if i == 0 else -sines
         table_ref[i, quarter:, width:] = -cosines if i == 0 else cosines
     real, imag = {}, {}
-    smooth = None
     for i in visit:
         if i % 2:
             table_copies[i].wait()
@@ -117,12 +115,9 @@
         spec = both[:256] + both[256:]
         real[i] = spec[:, :width]
         imag[i] = spec[:, width:]
-    for pair in ((0, 1), (2, 3)):
-        power = jnp.concatenate([real[k] * real[k] + imag[k] * imag[k] for k in pair], axis=1)
-        high, low = split(power)
-        rows = near[pair[0] * width : pair[0] * width + half]
-        part = dot(high, rows) + dot(low, rows)
-        smooth = part if smooth is None else smooth + part
+    power = jnp.concatenate([real[i] * real[i] + imag[i] * imag[i] for i in range(STEPS)], axis=1)
+    both = dot(jnp.concatenate(split(power), axis=0), near)
+    smooth = both[:256] + both[256:]
     order_copy.wait()
     factor = lax.rsqrt(smooth * share + 1e-06)
     channels = lax.broadcasted_iota(jnp.int32, (128, 128), 0)
@@ -220,17 +215,19 @@
     )(own, pair_count, *(in_hbm(x) for x in (pair_first.reshape(1, 256), pair_offset.reshape(1, 256), high, low)))
 
 
-def pairs_kernel(rim_ref, left_ref, right_ref, pick_ref, high_ref, low_ref, out_ref):
+def pairs_kernel(rim_ref, left_ref, right_ref, pick_ref, high_ref, low_ref, out_ref, rim_rows, parts_ref):
     apart = spread_matrix(8, True)
-    blocks = [dot(apart, rim_ref[b * 8 : b * 8 + 8].reshape(128, COLS)).astype(BF) for b in range(3)]
+    for b in range(3):
+        block = dot(apart, rim_ref[b * 8 : b * 8 + 8].reshape(128, COLS)).astype(BF)
+        for c in range(4):
+            for s in range(2):
+                at = (c * 2 + s) * 16
+                rim_rows[s, c, b * 16 : b * 16 + 16] = block[at : at + 16]
     pick = pick_ref[:, :REACH]
 
     def right(s, c):
-        at = (c * 2 + s) * 16
-        rim_rows = jnp.concatenate([block[at : at + 16] for block in blocks], axis=0)
-        return right_ref[s, c].astype(F32) + dot(pick, rim_rows)
-
-    highs, lows = {}, {}
+        return right_ref[s, c].astype(F32) + dot(pick, rim_rows[s, c])
+
     for c in range(2):
         re = im = None
         for s in range(2):
@@ -239,11 +236,10 @@
             one, two = a_re * c_re + a_im * c_im, a_im * c_re - a_re * c_im
             re = one if re is None else re + one
             im = two if im is None else im + two
-        highs[c], lows[c] = split(re)
-        highs[c + 2], lows[c + 2] = split(im)
-    high = jnp.concatenate([highs[c] for c in range(4)], axis=1)
-    low = jnp.concatenate([lows[c] for c in range(4)], axis=1)
-    total = dot(high, high_ref[...]) + dot(low, high_ref[...]) + dot(high, low_ref[...])
+        for part, at in ((re, c * COLS), (im, (c + 2) * COLS)):
+            parts_ref[:256, at : at + COLS], parts_ref[256:, at : at + COLS] = split(part)
+    both = dot(parts_ref[...], high_ref[...])
+    total = both[:256] + both[256:] + dot(parts_ref[:256], low_ref[...])
     out_ref[...] = total.astype(BF)
 
 
@@ -254,6 +250,7 @@
         in_specs=[vmem] * 6,
         out_specs=vmem,
         out_shape=jax.ShapeDtypeStruct((256, LAGS), BF),
+        scratch_shapes=[pltpu.VMEM((2, 4, REACH, COLS), BF), pltpu.VMEM((512, 2 * F), BF)],
         compiler_params=pltpu.CompilerParams(vmem_limit_bytes=32 * 1024 * 1024),
         name="pairs",
     )(rim, *parts)

time: 61 us -> 60.4 us (level)
  no operation moved by 1% of the time
where the time goes in v5:
time: 60.4 us; the launch traced here: 60.2 us
  blocking collectives  46.9 us (78%)
  Pallas kernels  7.03 us (12%)
  starting transfers between devices  3.07 us (5%)
  waiting for transfers between devices  1.91 us (3%)
  between operations  0.68 us (1%)
  other arithmetic  0.63 us (1%)
    all_to_all x1, blocking collectives, on_device(): own = lax.all_to_all(sent, 'chan', split_axis=0, concat_axis=0, tiled=True)  30.7 us
    all_to_all x1, blocking collectives, on_device(): lax.all_to_all(lags.reshape(groups, 256 // groups, LAGS), 'seg', 0, 0, ti...  16.2 us
    pallas_call x1, Pallas kernels, whitened(): pl.pallas_call(whiten_kernel, in_specs=[hbm] * 3, out_specs=pl.BlockSpec(...  4.14 us
    ppermute x1, starting transfers between devices, on_device(): lax.ppermute(own[:REACH // 2], 'chan', [(i + 1, i) for i in range(blocks...  3.07 us
    ppermute x1, waiting for transfers between devices, on_device(): lax.ppermute(own[:REACH // 2], 'chan', [(i + 1, i) for i in range(blocks...  1.91 us
    pallas_call x1, Pallas kernels, gathered(): pl.pallas_call(gather_kernel, in_specs=[vmem, pl.BlockSpec(memory_space=p...  1.57 us
    pallas_call x1, Pallas kernels, pair_lags(): pl.pallas_call(pairs_kernel, in_specs=[vmem] * 6, out_specs=vmem, out_sha...  1.32 us
  transfers between devices with their start and end apart: 1, of which 1 were waited for; matrix products, arithmetic and copies ran while one was open for 0% of the time, Pallas kernels for 3%

profile of v5, /device:TPU:5, one launch (start us, length us, event | category | flops | bytes accessed | tf_op | source)
XLA Modules:
  0.0 60.2 jit_solution(9566248616489548487)
XLA Ops:
  0.0 4.1 %whiten.1 = bf16[64,16,256]{2,1,0:T(8,128)(2,1)S(1)} custom-call(bf16[2,128,1536]{2,1,0:T(8,128)(2,1)} %raw_hbm.1, s32[1,128]{1,0:T(1,128)} %bitcast.7, bf16[4,384,256]{2,1,0:T(8,128)(2,1)} %constant.8.clone.table_hbm), custom_call_target="tpu_custom_call" | custom-call | tf_op jit(solution)/shard_map/whiten/pallas_call | solution.py:143
  4.1 30.7 %all_to_all.10.own_ref = bf16[64,16,256]{2,1,0:T(8,128)(2,1)S(1)} all-to-all(bf16[64,16,256]{2,1,0:T(8,128)(2,1)S(1)} %whiten.1), channel_id=1, replica_groups=mesh['chan'=64,'seg'=8] {'chan'}, dimensions={0} | all-to-all | bytes 1048576 | tf_op jit(solution)/shard_map/all_to_all | solution.py:264
  34.9 3.1 %collective-permute-start = (bf16[24,16,256]{2,1,0:T(8,128)(2,1)S(1)}, bf16[24,16,256]{2,1,0:T(8,128)(2,1)S(1)}, u32[]{:S(2)}, u32[]{:S(2)}) collective-permute-start(bf16[24,16,256]{2,1,0:T(8,128)(2,1)S(1)} %slice.4), channel_id=1, source_target_pairs={{8,0},{16,8},{24,16},{32,24},{40,32},{48,40},{56,48},{64,56},{72,6... | collective-permute-start | bytes 589832 | tf_op jit(solution)/shard_map/ppermute | solution.py:265
  38.6 1.6 %gather.1 = (bf16[2,4,256,256]{3,2,1,0:T(8,128)(2,1)S(1)}, bf16[2,4,256,256]{3,2,1,0:T(8,128)(2,1)S(1)}, bf16[256,128]{1,0:T(8,128)(2,1)S(1)}, bf16[1024,256]{1,0:T(8,128)(2,1)S(1)}, bf16[1024,256]{1,0:T(8,128)(2,1)S(1)}) custom-call(bf16[64,16,256]{2,1,0:T(8,128)(2,1)S(1)} %all_to_all.10.own_ref, s32[1]{0:T(128)S(6)} %copy.9.count_ref, s32[1,256]{1,0:T(1,128)} %bitcast.5, ...), custom_call_target="tpu_custom_call" | custom-call | tf_op jit(solution)/shard_map/gather/pallas_call | solution.py:202
  40.2 1.9 %collective-permute-done.rim_ref = bf16[24,16,256]{2,1,0:T(8,128)(2,1)S(1)} collective-permute-done((bf16[24,16,256]{2,1,0:T(8,128)(2,1)S(1)}, bf16[24,16,256]{2,1,0:T(8,128)(2,1)S(1)}, u32[]{:S(2)}, u32[]{:S(2)}) %collective-permute-start) | collective-permute-done | bytes 196640 | tf_op jit(solution)/shard_map/ppermute | solution.py:265
  42.1 1.3 %pairs.1 = bf16[256,256]{1,0:T(8,128)(2,1)S(1)} custom-call(bf16[24,16,256]{2,1,0:T(8,128)(2,1)S(1)} %collective-permute-done.rim_ref, bf16[2,4,256,256]{3,2,1,0:T(8,128)(2,1)S(1)} %get-tuple-element.10.left_ref, bf16[2,4,256,256]{3,2,1,0:T(8,128)(2,1)S(1)} %get-tuple-element.11.right_ref, bf16[256,128]{1,0:T(8,128)(2,1)S(1)} %get-tuple-element.12.pick_ref, ...), custom_call_target="tpu_custom_call" | custom-call | tf_op jit(solution)/shard_map/pairs/pallas_call | solution.py:248
  43.4 16.2 %all_to_all.11 = bf16[8,32,256]{2,1,0:T(8,128)(2,1)S(1)} all-to-all(bf16[8,32,256]{2,1,0:T(8,128)(2,1)S(1)} %bitcast.4), channel_id=1, replica_groups=mesh['chan'=64,'seg'=8] {'seg'}, dimensions={0} | all-to-all | bytes 262144 | tf_op jit(solution)/shard_map/all_to_all | solution.py:268
  59.6 0.6 %convert_reduce_fusion = f32[32,256]{1,0:T(8,128)} fusion(bf16[8,32,256]{2,1,0:T(8,128)(2,1)S(1)} %all_to_all.11), kind=kLoop, calls=%fused_computation | loop fusion | flops 122880 | bytes 163840 | tf_op jit(solution)/shard_map/reduce_sum | solution.py:269
  (1 shorter events, 0.0 us)
Async XLA Ops:
  34.9 7.2 %collective-permute-start = (bf16[24,16,256]{2,1,0:T(8,128)(2,1)S(1)}, bf16[24,16,256]{2,1,0:T(8,128)(2,1)S(1)}, u32[]{:S(2)}, u32[]{:S(2)}) collective-permute-start(bf16[24,16,256]{2,1,0:T(8,128)(2,1)S(1)} %slice.4), channel_id=1, source_target_pairs={{8,0},{16,8},{24,16},{32,24},{40,32},{48,40},{56,48},{64,56},{72,6... | collective-permute-start | bytes 589832 | tf_op jit(solution)/shard_map/ppermute | solution.py:265

commit v6 on v5

--- a/solution.py
+++ b/solution.py
@@ -27,7 +27,7 @@
     phase = (np.arange(quarter)[:, None] * BINS[None, :] % L).astype(np.float32) * np.float32(2.0 * math.pi / L)
     cosines = np.cos(phase).astype(BF).reshape(quarter, STEPS, F // STEPS)
     sines = (-np.sin(phase)).astype(BF).reshape(quarter, STEPS, F // STEPS)
-    return np.ascontiguousarray(np.concatenate([cosines, sines], axis=-1).transpose(1, 0, 2))
+    return np.concatenate([cosines, sines], axis=-1)[:, (0, 2, 1, 3)].reshape(quarter, 2 * F)
 
 
 def inverse_tables(factor):
@@ -73,13 +73,10 @@
 def whiten_kernel(raw_hbm, order_hbm, table_hbm, out_ref, raw_ref, order_ref, table_ref, even, odd, sems):
     width = F // STEPS
     quarter = L // 4
-    visit = (0, 2, 1, 3)
-    raw_copies = [pltpu.make_async_copy(raw_hbm.at[s], raw_ref.at[s], sems.at[s]) for s in range(2)]
-    table_copies = {
-        i: pltpu.make_async_copy(table_hbm.at[i], table_ref.at[i, :quarter], sems.at[2 + i]) for i in visit
-    }
-    order_copy = pltpu.make_async_copy(order_hbm, order_ref, sems.at[2 + STEPS])
-    for copy in (*raw_copies, *table_copies.values(), order_copy):
+    raw_copy = pltpu.make_async_copy(raw_hbm, raw_ref, sems.at[0])
+    table_copy = pltpu.make_async_copy(table_hbm, table_ref.at[:quarter], sems.at[1])
+    order_copy = pltpu.make_async_copy(order_hbm, order_ref, sems.at[2])
+    for copy in (raw_copy, table_copy, order_copy):
         copy.start()
     mix = spread_matrix(16, False)
 
@@ -92,32 +89,34 @@
     count = jnp.minimum(bin_line + BAND, F) - jnp.maximum(bin_line - BAND, 1) + 1
     share = 1.0 / count.astype(F32)
 
+    raw_copy.wait()
     for s in range(2):
-        raw_copies[s].wait()
-        for r in range(0, 128, 32):
-            wave = raw_ref[s, r : r + 32].astype(F32)
+        for r in range(0, 128, 16):
+            wave = raw_ref[s, r : r + 16].astype(F32)
             mean = jnp.sum(wave * wave, axis=-1, keepdims=True) * (1.0 / L)
             normed = (wave * lax.rsqrt(mean + 1e-05)).astype(BF).astype(F32)
             fold(normed, even, odd, s * 128 + r)
+    table_copy.wait()
+    specs = {}
+    for i in (1, 3):
+        at = 2 * COLS + (i // 2) * COLS
+        both = dot(even[i // 2], table_ref[:quarter, at : at + COLS])
+        specs[i] = both[:256] + both[256:]
+    for at in (0, COLS):
+        cosines = table_ref[:quarter, at : at + width]
+        sines = table_ref[:quarter, at + width : at + COLS]
+        table_ref[quarter:, at : at + width] = sines if at == 0 else -sines
+        table_ref[quarter:, at + width : at + COLS] = -cosines if at == 0 else cosines
+    both = dot(odd[...], table_ref[:, : 2 * COLS])
     for i in (0, 2):
-        table_copies[i].wait()
-        cosines = table_ref[i, :quarter, :width]
-        sines = table_ref[i, :quarter, width:]
-        table_ref[i, quarter:, :width] = sines if i == 0 else -sines
-        table_ref[i, quarter:, width:] = -cosines if i == 0 else cosines
+        at = (i // 2) * COLS
+        specs[i] = both[:256, at : at + COLS] + both[256:, at : at + COLS]
     real, imag = {}, {}
-    for i in visit:
-        if i % 2:
-            table_copies[i].wait()
-            both = dot(even[i // 2], table_ref[i, :quarter])
-        else:
-            both = dot(odd[...], table_ref[i])
-        spec = both[:256] + both[256:]
+    for i, spec in specs.items():
         real[i] = spec[:, :width]
         imag[i] = spec[:, width:]
     power = jnp.concatenate([real[i] * real[i] + imag[i] * imag[i] for i in range(STEPS)], axis=1)
-    both = dot(jnp.concatenate(split(power), axis=0), near)
-    smooth = both[:256] + both[256:]
+    smooth = dot(power.astype(BF), near)
     order_copy.wait()
     factor = lax.rsqrt(smooth * share + 1e-06)
     channels = lax.broadcasted_iota(jnp.int32, (128, 128), 0)
@@ -148,10 +147,10 @@
         scratch_shapes=[
             pltpu.VMEM((2, 128, L), BF),
             pltpu.VMEM((1, 128), jnp.int32),
-            pltpu.VMEM((STEPS, L // 2, COLS), BF),
+            pltpu.VMEM((L // 2, 2 * F), BF),
             pltpu.VMEM((2, 512, L // 4), BF),
             pltpu.VMEM((512, L // 2), BF),
-            pltpu.SemaphoreType.DMA((3 + STEPS,)),
+            pltpu.SemaphoreType.DMA((3,)),
         ],
         compiler_params=pltpu.CompilerParams(vmem_limit_bytes=32 * 1024 * 1024),
         name="whiten",

time: 60.4 us -> 59.8 us (0.990)
  Pallas kernels: 7.03 us -> 6.37 us
    pallas_call x1, Pallas kernels: 4.14 us -> 3.49 us  [whitened(): pl.pallas_call(whiten_kernel, in_specs=[hbm] * 3, out_specs=pl.BlockSpec(...]
where the time goes in v6:
time: 59.8 us; the launch traced here: 59.6 us
  blocking collectives  46.9 us (78%)
  Pallas kernels  6.37 us (11%)
  starting transfers between devices  3.07 us (5%)
  waiting for transfers between devices  1.91 us (3%)
  between operations  0.68 us (1%)
  other arithmetic  0.63 us (1%)
    all_to_all x1, blocking collectives, on_device(): own = lax.all_to_all(sent, 'chan', split_axis=0, concat_axis=0, tiled=True)  30.7 us
    all_to_all x1, blocking collectives, on_device(): lax.all_to_all(lags.reshape(groups, 256 // groups, LAGS), 'seg', 0, 0, ti...  16.2 us
    pallas_call x1, Pallas kernels, whitened(): pl.pallas_call(whiten_kernel, in_specs=[hbm] * 3, out_specs=pl.BlockSpec(...  3.49 us
    ppermute x1, starting transfers between devices, on_device(): lax.ppermute(own[:REACH // 2], 'chan', [(i + 1, i) for i in range(blocks...  3.07 us
    ppermute x1, waiting for transfers between devices, on_device(): lax.ppermute(own[:REACH // 2], 'chan', [(i + 1, i) for i in range(blocks...  1.91 us
    pallas_call x1, Pallas kernels, gathered(): pl.pallas_call(gather_kernel, in_specs=[vmem, pl.BlockSpec(memory_space=p...  1.57 us
    pallas_call x1, Pallas kernels, pair_lags(): pl.pallas_call(pairs_kernel, in_specs=[vmem] * 6, out_specs=vmem, out_sha...  1.32 us
  transfers between devices with their start and end apart: 1, of which 1 were waited for; matrix products, arithmetic and copies ran while one was open for 0% of the time, Pallas kernels for 3%

profile of v6, /device:TPU:5, one launch (start us, length us, event | category | flops | bytes accessed | tf_op | source)
XLA Modules:
  0.0 59.6 jit_solution(6041352730633911691)
XLA Ops:
  0.0 3.5 %whiten.1 = bf16[64,16,256]{2,1,0:T(8,128)(2,1)S(1)} custom-call(bf16[2,128,1536]{2,1,0:T(8,128)(2,1)} %raw_hbm.1, s32[1,128]{1,0:T(1,128)} %bitcast.7, bf16[384,1024]{1,0:T(8,128)(2,1)} %constant.8.clone.table_hbm), custom_call_target="tpu_custom_call" | custom-call | tf_op jit(solution)/shard_map/whiten/pallas_call | solution.py:142
  3.5 30.7 %all_to_all.10.own_ref = bf16[64,16,256]{2,1,0:T(8,128)(2,1)S(1)} all-to-all(bf16[64,16,256]{2,1,0:T(8,128)(2,1)S(1)} %whiten.1), channel_id=1, replica_groups=mesh['chan'=64,'seg'=8] {'chan'}, dimensions={0} | all-to-all | bytes 1048576 | tf_op jit(solution)/shard_map/all_to_all | solution.py:263
  34.2 3.1 %collective-permute-start = (bf16[24,16,256]{2,1,0:T(8,128)(2,1)S(1)}, bf16[24,16,256]{2,1,0:T(8,128)(2,1)S(1)}, u32[]{:S(2)}, u32[]{:S(2)}) collective-permute-start(bf16[24,16,256]{2,1,0:T(8,128)(2,1)S(1)} %slice.4), channel_id=1, source_target_pairs={{8,0},{16,8},{24,16},{32,24},{40,32},{48,40},{56,48},{64,56},{72,6... | collective-permute-start | bytes 589832 | tf_op jit(solution)/shard_map/ppermute | solution.py:264
  38.0 1.6 %gather.1 = (bf16[2,4,256,256]{3,2,1,0:T(8,128)(2,1)S(1)}, bf16[2,4,256,256]{3,2,1,0:T(8,128)(2,1)S(1)}, bf16[256,128]{1,0:T(8,128)(2,1)S(1)}, bf16[1024,256]{1,0:T(8,128)(2,1)S(1)}, bf16[1024,256]{1,0:T(8,128)(2,1)S(1)}) custom-call(bf16[64,16,256]{2,1,0:T(8,128)(2,1)S(1)} %all_to_all.10.own_ref, s32[1]{0:T(128)S(6)} %copy.9.count_ref, s32[1,256]{1,0:T(1,128)} %bitcast.5, ...), custom_call_target="tpu_custom_call" | custom-call | tf_op jit(solution)/shard_map/gather/pallas_call | solution.py:201
  39.5 1.9 %collective-permute-done.rim_ref = bf16[24,16,256]{2,1,0:T(8,128)(2,1)S(1)} collective-permute-done((bf16[24,16,256]{2,1,0:T(8,128)(2,1)S(1)}, bf16[24,16,256]{2,1,0:T(8,128)(2,1)S(1)}, u32[]{:S(2)}, u32[]{:S(2)}) %collective-permute-start) | collective-permute-done | bytes 196640 | tf_op jit(solution)/shard_map/ppermute | solution.py:264
  41.4 1.3 %pairs.1 = bf16[256,256]{1,0:T(8,128)(2,1)S(1)} custom-call(bf16[24,16,256]{2,1,0:T(8,128)(2,1)S(1)} %collective-permute-done.rim_ref, bf16[2,4,256,256]{3,2,1,0:T(8,128)(2,1)S(1)} %get-tuple-element.10.left_ref, bf16[2,4,256,256]{3,2,1,0:T(8,128)(2,1)S(1)} %get-tuple-element.11.right_ref, bf16[256,128]{1,0:T(8,128)(2,1)S(1)} %get-tuple-element.12.pick_ref, ...), custom_call_target="tpu_custom_call" | custom-call | tf_op jit(solution)/shard_map/pairs/pallas_call | solution.py:247
  42.8 16.2 %all_to_all.11 = bf16[8,32,256]{2,1,0:T(8,128)(2,1)S(1)} all-to-all(bf16[8,32,256]{2,1,0:T(8,128)(2,1)S(1)} %bitcast.4), channel_id=1, replica_groups=mesh['chan'=64,'seg'=8] {'seg'}, dimensions={0} | all-to-all | bytes 262144 | tf_op jit(solution)/shard_map/all_to_all | solution.py:267
  59.0 0.6 %convert_reduce_fusion = f32[32,256]{1,0:T(8,128)} fusion(bf16[8,32,256]{2,1,0:T(8,128)(2,1)S(1)} %all_to_all.11), kind=kLoop, calls=%fused_computation | loop fusion | flops 122880 | bytes 163840 | tf_op jit(solution)/shard_map/reduce_sum | solution.py:268
  (1 shorter events, 0.0 us)
Async XLA Ops:
  34.2 7.2 %collective-permute-start = (bf16[24,16,256]{2,1,0:T(8,128)(2,1)S(1)}, bf16[24,16,256]{2,1,0:T(8,128)(2,1)S(1)}, u32[]{:S(2)}, u32[]{:S(2)}) collective-permute-start(bf16[24,16,256]{2,1,0:T(8,128)(2,1)S(1)} %slice.4), channel_id=1, source_target_pairs={{8,0},{16,8},{24,16},{32,24},{40,32},{48,40},{56,48},{64,56},{72,6... | collective-permute-start | bytes 589832 | tf_op jit(solution)/shard_map/ppermute | solution.py:264

commit v7 on v6

--- a/solution.py
+++ b/solution.py
@@ -76,7 +76,7 @@
     raw_copy = pltpu.make_async_copy(raw_hbm, raw_ref, sems.at[0])
     table_copy = pltpu.make_async_copy(table_hbm, table_ref.at[:quarter], sems.at[1])
     order_copy = pltpu.make_async_copy(order_hbm, order_ref, sems.at[2])
-    for copy in (raw_copy, table_copy, order_copy):
+    for copy in (order_copy, raw_copy, table_copy):
         copy.start()
     mix = spread_matrix(16, False)
 
@@ -89,14 +89,17 @@
     count = jnp.minimum(bin_line + BAND, F) - jnp.maximum(bin_line - BAND, 1) + 1
     share = 1.0 / count.astype(F32)
 
+    order_copy.wait()
+    channels = lax.broadcasted_iota(jnp.int32, (128, 128), 0)
+    pick = (channels == order_ref[...]).astype(F32).T.astype(BF)
     raw_copy.wait()
+    table_copy.wait()
     for s in range(2):
         for r in range(0, 128, 16):
             wave = raw_ref[s, r : r + 16].astype(F32)
             mean = jnp.sum(wave * wave, axis=-1, keepdims=True) * (1.0 / L)
             normed = (wave * lax.rsqrt(mean + 1e-05)).astype(BF).astype(F32)
             fold(normed, even, odd, s * 128 + r)
-    table_copy.wait()
     specs = {}
     for i in (1, 3):
         at = 2 * COLS + (i // 2) * COLS
@@ -117,10 +120,7 @@
         imag[i] = spec[:, width:]
     power = jnp.concatenate([real[i] * real[i] + imag[i] * imag[i] for i in range(STEPS)], axis=1)
     smooth = dot(power.astype(BF), near)
-    order_copy.wait()
     factor = lax.rsqrt(smooth * share + 1e-06)
-    channels = lax.broadcasted_iota(jnp.int32, (128, 128), 0)
-    pick = (channels == order_ref[...]).astype(F32).T.astype(BF)
     picked = []
     for s in range(2):
         rows = slice(s * 128, s * 128 + 128)

time: 59.8 us -> 59.7 us (level)
  no operation moved by 1% of the time
where the time goes in v7:
time: 59.7 us; the launch traced here: 59.5 us
  blocking collectives  46.9 us (79%)
  Pallas kernels  6.26 us (10%)
  starting transfers between devices  3.07 us (5%)
  waiting for transfers between devices  1.91 us (3%)
  between operations  0.68 us (1%)
  other arithmetic  0.63 us (1%)
    all_to_all x1, blocking collectives, on_device(): own = lax.all_to_all(sent, 'chan', split_axis=0, concat_axis=0, tiled=True)  30.7 us
    all_to_all x1, blocking collectives, on_device(): lax.all_to_all(lags.reshape(groups, 256 // groups, LAGS), 'seg', 0, 0, ti...  16.2 us
    pallas_call x1, Pallas kernels, whitened(): pl.pallas_call(whiten_kernel, in_specs=[hbm] * 3, out_specs=pl.BlockSpec(...  3.37 us
    ppermute x1, starting transfers between devices, on_device(): lax.ppermute(own[:REACH // 2], 'chan', [(i + 1, i) for i in range(blocks...  3.07 us
    ppermute x1, waiting for transfers between devices, on_device(): lax.ppermute(own[:REACH // 2], 'chan', [(i + 1, i) for i in range(blocks...  1.91 us
    pallas_call x1, Pallas kernels, gathered(): pl.pallas_call(gather_kernel, in_specs=[vmem, pl.BlockSpec(memory_space=p...  1.57 us
    pallas_call x1, Pallas kernels, pair_lags(): pl.pallas_call(pairs_kernel, in_specs=[vmem] * 6, out_specs=vmem, out_sha...  1.32 us
  transfers between devices with their start and end apart: 1, of which 1 were waited for; matrix products, arithmetic and copies ran while one was open for 0% of the time, Pallas kernels for 3%

profile of v7, /device:TPU:5, one launch (start us, length us, event | category | flops | bytes accessed | tf_op | source)
XLA Modules:
  0.0 59.5 jit_solution(5235991688281084639)
XLA Ops:
  0.0 3.4 %whiten.1 = bf16[64,16,256]{2,1,0:T(8,128)(2,1)S(1)} custom-call(bf16[2,128,1536]{2,1,0:T(8,128)(2,1)} %raw_hbm.1, s32[1,128]{1,0:T(1,128)} %bitcast.7, bf16[384,1024]{1,0:T(8,128)(2,1)} %constant.8.clone.table_hbm), custom_call_target="tpu_custom_call" | custom-call | tf_op jit(solution)/shard_map/whiten/pallas_call | solution.py:142
  3.4 30.7 %all_to_all.10.own_ref = bf16[64,16,256]{2,1,0:T(8,128)(2,1)S(1)} all-to-all(bf16[64,16,256]{2,1,0:T(8,128)(2,1)S(1)} %whiten.1), channel_id=1, replica_groups=mesh['chan'=64,'seg'=8] {'chan'}, dimensions={0} | all-to-all | bytes 1048576 | tf_op jit(solution)/shard_map/all_to_all | solution.py:263
  34.1 3.1 %collective-permute-start = (bf16[24,16,256]{2,1,0:T(8,128)(2,1)S(1)}, bf16[24,16,256]{2,1,0:T(8,128)(2,1)S(1)}, u32[]{:S(2)}, u32[]{:S(2)}) collective-permute-start(bf16[24,16,256]{2,1,0:T(8,128)(2,1)S(1)} %slice.4), channel_id=1, source_target_pairs={{8,0},{16,8},{24,16},{32,24},{40,32},{48,40},{56,48},{64,56},{72,6... | collective-permute-start | bytes 589832 | tf_op jit(solution)/shard_map/ppermute | solution.py:264
  37.8 1.6 %gather.1 = (bf16[2,4,256,256]{3,2,1,0:T(8,128)(2,1)S(1)}, bf16[2,4,256,256]{3,2,1,0:T(8,128)(2,1)S(1)}, bf16[256,128]{1,0:T(8,128)(2,1)S(1)}, bf16[1024,256]{1,0:T(8,128)(2,1)S(1)}, bf16[1024,256]{1,0:T(8,128)(2,1)S(1)}) custom-call(bf16[64,16,256]{2,1,0:T(8,128)(2,1)S(1)} %all_to_all.10.own_ref, s32[1]{0:T(128)S(6)} %copy.9.count_ref, s32[1,256]{1,0:T(1,128)} %bitcast.5, ...), custom_call_target="tpu_custom_call" | custom-call | tf_op jit(solution)/shard_map/gather/pallas_call | solution.py:201
  39.4 1.9 %collective-permute-done.rim_ref = bf16[24,16,256]{2,1,0:T(8,128)(2,1)S(1)} collective-permute-done((bf16[24,16,256]{2,1,0:T(8,128)(2,1)S(1)}, bf16[24,16,256]{2,1,0:T(8,128)(2,1)S(1)}, u32[]{:S(2)}, u32[]{:S(2)}) %collective-permute-start) | collective-permute-done | bytes 196640 | tf_op jit(solution)/shard_map/ppermute | solution.py:264
  41.3 1.3 %pairs.1 = bf16[256,256]{1,0:T(8,128)(2,1)S(1)} custom-call(bf16[24,16,256]{2,1,0:T(8,128)(2,1)S(1)} %collective-permute-done.rim_ref, bf16[2,4,256,256]{3,2,1,0:T(8,128)(2,1)S(1)} %get-tuple-element.10.left_ref, bf16[2,4,256,256]{3,2,1,0:T(8,128)(2,1)S(1)} %get-tuple-element.11.right_ref, bf16[256,128]{1,0:T(8,128)(2,1)S(1)} %get-tuple-element.12.pick_ref, ...), custom_call_target="tpu_custom_call" | custom-call | tf_op jit(solution)/shard_map/pairs/pallas_call | solution.py:247
  42.6 16.2 %all_to_all.11 = bf16[8,32,256]{2,1,0:T(8,128)(2,1)S(1)} all-to-all(bf16[8,32,256]{2,1,0:T(8,128)(2,1)S(1)} %bitcast.4), channel_id=1, replica_groups=mesh['chan'=64,'seg'=8] {'seg'}, dimensions={0} | all-to-all | bytes 262144 | tf_op jit(solution)/shard_map/all_to_all | solution.py:267
  58.8 0.6 %convert_reduce_fusion = f32[32,256]{1,0:T(8,128)} fusion(bf16[8,32,256]{2,1,0:T(8,128)(2,1)S(1)} %all_to_all.11), kind=kLoop, calls=%fused_computation | loop fusion | flops 122880 | bytes 163840 | tf_op jit(solution)/shard_map/reduce_sum | solution.py:268
  (1 shorter events, 0.0 us)
Async XLA Ops:
  34.1 7.2 %collective-permute-start = (bf16[24,16,256]{2,1,0:T(8,128)(2,1)S(1)}, bf16[24,16,256]{2,1,0:T(8,128)(2,1)S(1)}, u32[]{:S(2)}, u32[]{:S(2)}) collective-permute-start(bf16[24,16,256]{2,1,0:T(8,128)(2,1)S(1)} %slice.4), channel_id=1, source_target_pairs={{8,0},{16,8},{24,16},{32,24},{40,32},{48,40},{56,48},{64,56},{72,6... | collective-permute-start | bytes 589832 | tf_op jit(solution)/shard_map/ppermute | solution.py:264

commit v8 on v7

--- a/solution.py
+++ b/solution.py
@@ -64,7 +64,7 @@
     count = normed.shape[0]
     upper, lower = slice(first_row, first_row + count), slice(first_row + 256, first_row + 256 + count)
     for at, value in enumerate((even0 - even1, even0 + even1)):
-        even[at, upper], even[at, lower] = split(value)
+        even[at, upper, :quarter], even[at, upper, quarter:] = split(value)
     for side, value in enumerate((x0 - x2, x1 - x3)):
         columns = slice(side * quarter, (side + 1) * quarter)
         odd[upper, columns], odd[lower, columns] = split(value)
@@ -73,10 +73,10 @@
 def whiten_kernel(raw_hbm, order_hbm, table_hbm, out_ref, raw_ref, order_ref, table_ref, even, odd, sems):
     width = F // STEPS
     quarter = L // 4
-    raw_copy = pltpu.make_async_copy(raw_hbm, raw_ref, sems.at[0])
+    raw_copies = [pltpu.make_async_copy(raw_hbm.at[s], raw_ref.at[s], sems.at[3 * s]) for s in range(2)]
     table_copy = pltpu.make_async_copy(table_hbm, table_ref.at[:quarter], sems.at[1])
     order_copy = pltpu.make_async_copy(order_hbm, order_ref, sems.at[2])
-    for copy in (order_copy, raw_copy, table_copy):
+    for copy in (order_copy, *raw_copies, table_copy):
         copy.start()
     mix = spread_matrix(16, False)
 
@@ -92,9 +92,10 @@
     order_copy.wait()
     channels = lax.broadcasted_iota(jnp.int32, (128, 128), 0)
     pick = (channels == order_ref[...]).astype(F32).T.astype(BF)
-    raw_copy.wait()
-    table_copy.wait()
     for s in range(2):
+        raw_copies[s].wait()
+        if s == 1:
+            table_copy.wait()
         for r in range(0, 128, 16):
             wave = raw_ref[s, r : r + 16].astype(F32)
             mean = jnp.sum(wave * wave, axis=-1, keepdims=True) * (1.0 / L)
@@ -103,8 +104,8 @@
     specs = {}
     for i in (1, 3):
         at = 2 * COLS + (i // 2) * COLS
-        both = dot(even[i // 2], table_ref[:quarter, at : at + COLS])
-        specs[i] = both[:256] + both[256:]
+        table_ref[quarter:, at : at + COLS] = table_ref[:quarter, at : at + COLS]
+        specs[i] = dot(even[i // 2], table_ref[:, at : at + COLS])
     for at in (0, COLS):
         cosines = table_ref[:quarter, at : at + width]
         sines = table_ref[:quarter, at + width : at + COLS]
@@ -148,9 +149,9 @@
             pltpu.VMEM((2, 128, L), BF),
             pltpu.VMEM((1, 128), jnp.int32),
             pltpu.VMEM((L // 2, 2 * F), BF),
-            pltpu.VMEM((2, 512, L // 4), BF),
+            pltpu.VMEM((2, 256, L // 2), BF),
             pltpu.VMEM((512, L // 2), BF),
-            pltpu.SemaphoreType.DMA((3,)),
+            pltpu.SemaphoreType.DMA((4,)),
         ],
         compiler_params=pltpu.CompilerParams(vmem_limit_bytes=32 * 1024 * 1024),
         name="whiten",

time: 59.7 us -> 59.5 us (level)
  no operation moved by 1% of the time
where the time goes in v8:
time: 59.5 us; the launch traced here: 59.2 us
  blocking collectives  46.9 us (79%)
  Pallas kernels  6.01 us (10%)
  starting transfers between devices  3.07 us (5%)
  waiting for transfers between devices  1.91 us (3%)
  between operations  0.68 us (1%)
  other arithmetic  0.63 us (1%)
    all_to_all x1, blocking collectives, on_device(): own = lax.all_to_all(sent, 'chan', split_axis=0, concat_axis=0, tiled=True)  30.7 us
    all_to_all x1, blocking collectives, on_device(): lax.all_to_all(lags.reshape(groups, 256 // groups, LAGS), 'seg', 0, 0, ti...  16.2 us
    pallas_call x1, Pallas kernels, whitened(): pl.pallas_call(whiten_kernel, in_specs=[hbm] * 3, out_specs=pl.BlockSpec(...  3.13 us
    ppermute x1, starting transfers between devices, on_device(): lax.ppermute(own[:REACH // 2], 'chan', [(i + 1, i) for i in range(blocks...  3.07 us
    ppermute x1, waiting for transfers between devices, on_device(): lax.ppermute(own[:REACH // 2], 'chan', [(i + 1, i) for i in range(blocks...  1.91 us
    pallas_call x1, Pallas kernels, gathered(): pl.pallas_call(gather_kernel, in_specs=[vmem, pl.BlockSpec(memory_space=p...  1.57 us
    pallas_call x1, Pallas kernels, pair_lags(): pl.pallas_call(pairs_kernel, in_specs=[vmem] * 6, out_specs=vmem, out_sha...  1.32 us
  transfers between devices with their start and end apart: 1, of which 1 were waited for; matrix products, arithmetic and copies ran while one was open for 0% of the time, Pallas kernels for 3%

profile of v8, /device:TPU:5, one launch (start us, length us, event | category | flops | bytes accessed | tf_op | source)
XLA Modules:
  0.0 59.2 jit_solution(12773755471036693962)
XLA Ops:
  0.0 3.1 %whiten.1 = bf16[64,16,256]{2,1,0:T(8,128)(2,1)S(1)} custom-call(bf16[2,128,1536]{2,1,0:T(8,128)(2,1)} %raw_hbm.1, s32[1,128]{1,0:T(1,128)} %bitcast.7, bf16[384,1024]{1,0:T(8,128)(2,1)} %constant.8.clone.table_hbm), custom_call_target="tpu_custom_call" | custom-call | tf_op jit(solution)/shard_map/whiten/pallas_call | solution.py:143
  3.1 30.7 %all_to_all.10.own_ref = bf16[64,16,256]{2,1,0:T(8,128)(2,1)S(1)} all-to-all(bf16[64,16,256]{2,1,0:T(8,128)(2,1)S(1)} %whiten.1), channel_id=1, replica_groups=mesh['chan'=64,'seg'=8] {'chan'}, dimensions={0} | all-to-all | bytes 1048576 | tf_op jit(solution)/shard_map/all_to_all | solution.py:264
  33.9 3.1 %collective-permute-start = (bf16[24,16,256]{2,1,0:T(8,128)(2,1)S(1)}, bf16[24,16,256]{2,1,0:T(8,128)(2,1)S(1)}, u32[]{:S(2)}, u32[]{:S(2)}) collective-permute-start(bf16[24,16,256]{2,1,0:T(8,128)(2,1)S(1)} %slice.4), channel_id=1, source_target_pairs={{8,0},{16,8},{24,16},{32,24},{40,32},{48,40},{56,48},{64,56},{72,6... | collective-permute-start | bytes 589832 | tf_op jit(solution)/shard_map/ppermute | solution.py:265
  37.6 1.6 %gather.1 = (bf16[2,4,256,256]{3,2,1,0:T(8,128)(2,1)S(1)}, bf16[2,4,256,256]{3,2,1,0:T(8,128)(2,1)S(1)}, bf16[256,128]{1,0:T(8,128)(2,1)S(1)}, bf16[1024,256]{1,0:T(8,128)(2,1)S(1)}, bf16[1024,256]{1,0:T(8,128)(2,1)S(1)}) custom-call(bf16[64,16,256]{2,1,0:T(8,128)(2,1)S(1)} %all_to_all.10.own_ref, s32[1]{0:T(128)S(6)} %copy.9.count_ref, s32[1,256]{1,0:T(1,128)} %bitcast.5, ...), custom_call_target="tpu_custom_call" | custom-call | tf_op jit(solution)/shard_map/gather/pallas_call | solution.py:202
  39.2 1.9 %collective-permute-done.rim_ref = bf16[24,16,256]{2,1,0:T(8,128)(2,1)S(1)} collective-permute-done((bf16[24,16,256]{2,1,0:T(8,128)(2,1)S(1)}, bf16[24,16,256]{2,1,0:T(8,128)(2,1)S(1)}, u32[]{:S(2)}, u32[]{:S(2)}) %collective-permute-start) | collective-permute-done | bytes 196640 | tf_op jit(solution)/shard_map/ppermute | solution.py:265
  41.1 1.3 %pairs.1 = bf16[256,256]{1,0:T(8,128)(2,1)S(1)} custom-call(bf16[24,16,256]{2,1,0:T(8,128)(2,1)S(1)} %collective-permute-done.rim_ref, bf16[2,4,256,256]{3,2,1,0:T(8,128)(2,1)S(1)} %get-tuple-element.10.left_ref, bf16[2,4,256,256]{3,2,1,0:T(8,128)(2,1)S(1)} %get-tuple-element.11.right_ref, bf16[256,128]{1,0:T(8,128)(2,1)S(1)} %get-tuple-element.12.pick_ref, ...), custom_call_target="tpu_custom_call" | custom-call | tf_op jit(solution)/shard_map/pairs/pallas_call | solution.py:248
  42.4 16.2 %all_to_all.11 = bf16[8,32,256]{2,1,0:T(8,128)(2,1)S(1)} all-to-all(bf16[8,32,256]{2,1,0:T(8,128)(2,1)S(1)} %bitcast.4), channel_id=1, replica_groups=mesh['chan'=64,'seg'=8] {'seg'}, dimensions={0} | all-to-all | bytes 262144 | tf_op jit(solution)/shard_map/all_to_all | solution.py:268
  58.6 0.6 %convert_reduce_fusion = f32[32,256]{1,0:T(8,128)} fusion(bf16[8,32,256]{2,1,0:T(8,128)(2,1)S(1)} %all_to_all.11), kind=kLoop, calls=%fused_computation | loop fusion | flops 122880 | bytes 163840 | tf_op jit(solution)/shard_map/reduce_sum | solution.py:269
  (1 shorter events, 0.0 us)
Async XLA Ops:
  33.9 7.2 %collective-permute-start = (bf16[24,16,256]{2,1,0:T(8,128)(2,1)S(1)}, bf16[24,16,256]{2,1,0:T(8,128)(2,1)S(1)}, u32[]{:S(2)}, u32[]{:S(2)}) collective-permute-start(bf16[24,16,256]{2,1,0:T(8,128)(2,1)S(1)} %slice.4), channel_id=1, source_target_pairs={{8,0},{16,8},{24,16},{32,24},{40,32},{48,40},{56,48},{64,56},{72,6... | collective-permute-start | bytes 589832 | tf_op jit(solution)/shard_map/ppermute | solution.py:265

commit v9 on v8

--- a/solution.py
+++ b/solution.py
@@ -76,7 +76,7 @@
     raw_copies = [pltpu.make_async_copy(raw_hbm.at[s], raw_ref.at[s], sems.at[3 * s]) for s in range(2)]
     table_copy = pltpu.make_async_copy(table_hbm, table_ref.at[:quarter], sems.at[1])
     order_copy = pltpu.make_async_copy(order_hbm, order_ref, sems.at[2])
-    for copy in (order_copy, *raw_copies, table_copy):
+    for copy in (order_copy, raw_copies[0], table_copy, raw_copies[1]):
         copy.start()
     mix = spread_matrix(16, False)
 
@@ -94,23 +94,24 @@
     pick = (channels == order_ref[...]).astype(F32).T.astype(BF)
     for s in range(2):
         raw_copies[s].wait()
-        if s == 1:
-            table_copy.wait()
         for r in range(0, 128, 16):
             wave = raw_ref[s, r : r + 16].astype(F32)
             mean = jnp.sum(wave * wave, axis=-1, keepdims=True) * (1.0 / L)
             normed = (wave * lax.rsqrt(mean + 1e-05)).astype(BF).astype(F32)
             fold(normed, even, odd, s * 128 + r)
+        if s == 0:
+            table_copy.wait()
+            for at in (2 * COLS, 3 * COLS):
+                table_ref[quarter:, at : at + COLS] = table_ref[:quarter, at : at + COLS]
+            for at in (0, COLS):
+                cosines = table_ref[:quarter, at : at + width]
+                sines = table_ref[:quarter, at + width : at + COLS]
+                table_ref[quarter:, at : at + width] = sines if at == 0 else -sines
+                table_ref[quarter:, at + width : at + COLS] = -cosines if at == 0 else cosines
     specs = {}
     for i in (1, 3):
         at = 2 * COLS + (i // 2) * COLS
-        table_ref[quarter:, at : at + COLS] = table_ref[:quarter, at : at + COLS]
         specs[i] = dot(even[i // 2], table_ref[:, at : at + COLS])
-    for at in (0, COLS):
-        cosines = table_ref[:quarter, at : at + width]
-        sines = table_ref[:quarter, at + width : at + COLS]
-        table_ref[quarter:, at : at + width] = sines if at == 0 else -sines
-        table_ref[quarter:, at + width : at + COLS] = -cosines if at == 0 else cosines
     both = dot(odd[...], table_ref[:, : 2 * COLS])
     for i in (0, 2):
         at = (i // 2) * COLS

time: 59.5 us -> 59.5 us (level)
  no operation moved by 1% of the time
where the time goes in v9:
time: 59.5 us; the launch traced here: 59.3 us
  blocking collectives  46.9 us (79%)
  Pallas kernels  6.04 us (10%)
  starting transfers between devices  3.07 us (5%)
  waiting for transfers between devices  1.91 us (3%)
  between operations  0.68 us (1%)
  other arithmetic  0.63 us (1%)
    all_to_all x1, blocking collectives, on_device(): own = lax.all_to_all(sent, 'chan', split_axis=0, concat_axis=0, tiled=True)  30.7 us
    all_to_all x1, blocking collectives, on_device(): lax.all_to_all(lags.reshape(groups, 256 // groups, LAGS), 'seg', 0, 0, ti...  16.2 us
    pallas_call x1, Pallas kernels, whitened(): pl.pallas_call(whiten_kernel, in_specs=[hbm] * 3, out_specs=pl.BlockSpec(...  3.16 us
    ppermute x1, starting transfers between devices, on_device(): lax.ppermute(own[:REACH // 2], 'chan', [(i + 1, i) for i in range(blocks...  3.07 us
    ppermute x1, waiting for transfers between devices, on_device(): lax.ppermute(own[:REACH // 2], 'chan', [(i + 1, i) for i in range(blocks...  1.91 us
    pallas_call x1, Pallas kernels, gathered(): pl.pallas_call(gather_kernel, in_specs=[vmem, pl.BlockSpec(memory_space=p...  1.57 us
    pallas_call x1, Pallas kernels, pair_lags(): pl.pallas_call(pairs_kernel, in_specs=[vmem] * 6, out_specs=vmem, out_sha...  1.32 us
  transfers between devices with their start and end apart: 1, of which 1 were waited for; matrix products, arithmetic and copies ran while one was open for 0% of the time, Pallas kernels for 3%

profile of v9, /device:TPU:5, one launch (start us, length us, event | category | flops | bytes accessed | tf_op | source)
XLA Modules:
  0.0 59.3 jit_solution(11621279085043864830)
XLA Ops:
  0.0 3.2 %whiten.1 = bf16[64,16,256]{2,1,0:T(8,128)(2,1)S(1)} custom-call(bf16[2,128,1536]{2,1,0:T(8,128)(2,1)} %raw_hbm.1, s32[1,128]{1,0:T(1,128)} %bitcast.7, bf16[384,1024]{1,0:T(8,128)(2,1)} %constant.8.clone.table_hbm), custom_call_target="tpu_custom_call" | custom-call | tf_op jit(solution)/shard_map/whiten/pallas_call | solution.py:144
  3.2 30.7 %all_to_all.10.own_ref = bf16[64,16,256]{2,1,0:T(8,128)(2,1)S(1)} all-to-all(bf16[64,16,256]{2,1,0:T(8,128)(2,1)S(1)} %whiten.1), channel_id=1, replica_groups=mesh['chan'=64,'seg'=8] {'chan'}, dimensions={0} | all-to-all | bytes 1048576 | tf_op jit(solution)/shard_map/all_to_all | solution.py:265
  33.9 3.1 %collective-permute-start = (bf16[24,16,256]{2,1,0:T(8,128)(2,1)S(1)}, bf16[24,16,256]{2,1,0:T(8,128)(2,1)S(1)}, u32[]{:S(2)}, u32[]{:S(2)}) collective-permute-start(bf16[24,16,256]{2,1,0:T(8,128)(2,1)S(1)} %slice.4), channel_id=1, source_target_pairs={{8,0},{16,8},{24,16},{32,24},{40,32},{48,40},{56,48},{64,56},{72,6... | collective-permute-start | bytes 589832 | tf_op jit(solution)/shard_map/ppermute | solution.py:266
  37.6 1.6 %gather.1 = (bf16[2,4,256,256]{3,2,1,0:T(8,128)(2,1)S(1)}, bf16[2,4,256,256]{3,2,1,0:T(8,128)(2,1)S(1)}, bf16[256,128]{1,0:T(8,128)(2,1)S(1)}, bf16[1024,256]{1,0:T(8,128)(2,1)S(1)}, bf16[1024,256]{1,0:T(8,128)(2,1)S(1)}) custom-call(bf16[64,16,256]{2,1,0:T(8,128)(2,1)S(1)} %all_to_all.10.own_ref, s32[1]{0:T(128)S(6)} %copy.9.count_ref, s32[1,256]{1,0:T(1,128)} %bitcast.5, ...), custom_call_target="tpu_custom_call" | custom-call | tf_op jit(solution)/shard_map/gather/pallas_call | solution.py:203
  39.2 1.9 %collective-permute-done.rim_ref = bf16[24,16,256]{2,1,0:T(8,128)(2,1)S(1)} collective-permute-done((bf16[24,16,256]{2,1,0:T(8,128)(2,1)S(1)}, bf16[24,16,256]{2,1,0:T(8,128)(2,1)S(1)}, u32[]{:S(2)}, u32[]{:S(2)}) %collective-permute-start) | collective-permute-done | bytes 196640 | tf_op jit(solution)/shard_map/ppermute | solution.py:266
  41.1 1.3 %pairs.1 = bf16[256,256]{1,0:T(8,128)(2,1)S(1)} custom-call(bf16[24,16,256]{2,1,0:T(8,128)(2,1)S(1)} %collective-permute-done.rim_ref, bf16[2,4,256,256]{3,2,1,0:T(8,128)(2,1)S(1)} %get-tuple-element.10.left_ref, bf16[2,4,256,256]{3,2,1,0:T(8,128)(2,1)S(1)} %get-tuple-element.11.right_ref, bf16[256,128]{1,0:T(8,128)(2,1)S(1)} %get-tuple-element.12.pick_ref, ...), custom_call_target="tpu_custom_call" | custom-call | tf_op jit(solution)/shard_map/pairs/pallas_call | solution.py:249
  42.4 16.2 %all_to_all.11 = bf16[8,32,256]{2,1,0:T(8,128)(2,1)S(1)} all-to-all(bf16[8,32,256]{2,1,0:T(8,128)(2,1)S(1)} %bitcast.4), channel_id=1, replica_groups=mesh['chan'=64,'seg'=8] {'seg'}, dimensions={0} | all-to-all | bytes 262144 | tf_op jit(solution)/shard_map/all_to_all | solution.py:269
  58.6 0.6 %convert_reduce_fusion = f32[32,256]{1,0:T(8,128)} fusion(bf16[8,32,256]{2,1,0:T(8,128)(2,1)S(1)} %all_to_all.11), kind=kLoop, calls=%fused_computation | loop fusion | flops 122880 | bytes 163840 | tf_op jit(solution)/shard_map/reduce_sum | solution.py:270
  (1 shorter events, 0.0 us)
Async XLA Ops:
  33.9 7.2 %collective-permute-start = (bf16[24,16,256]{2,1,0:T(8,128)(2,1)S(1)}, bf16[24,16,256]{2,1,0:T(8,128)(2,1)S(1)}, u32[]{:S(2)}, u32[]{:S(2)}) collective-permute-start(bf16[24,16,256]{2,1,0:T(8,128)(2,1)S(1)} %slice.4), channel_id=1, source_target_pairs={{8,0},{16,8},{24,16},{32,24},{40,32},{48,40},{56,48},{64,56},{72,6... | collective-permute-start | bytes 589832 | tf_op jit(solution)/shard_map/ppermute | solution.py:266

commit v10 on v9

--- a/solution.py
+++ b/solution.py
@@ -161,8 +161,8 @@
 
 def gather_kernel(
     own_ref, count_ref, first_hbm, offset_hbm, high_hbm, low_hbm,
-    left_ref, right_ref, pick_ref, high_ref, low_ref,
-    rows_ref, first_ref, offset_ref, sems,
+    left_ref, rows_ref, pick_ref, high_ref, low_ref,
+    first_ref, offset_ref, sems,
 ):
     moves = ((first_hbm, first_ref), (offset_hbm, offset_ref), (high_hbm, high_ref), (low_hbm, low_ref))
     copies = [pltpu.make_async_copy(src, dst, sems.at[i]) for i, (src, dst) in enumerate(moves)]
@@ -183,13 +183,11 @@
     live_first = jnp.where(slot < count_ref[0], first, -1)
     at = lax.broadcasted_iota(jnp.int32, (128, 256), 0)
     left_pick = (at == live_first).astype(F32).T.astype(BF)
-    right_pick = (at == second).astype(F32).T.astype(BF)
-    pick_ref[...] = (at + 128 == second).astype(F32).T.astype(BF)
+    any_at = lax.broadcasted_iota(jnp.int32, (128 + REACH, 256), 0)
+    pick_ref[...] = (any_at == second).astype(F32).T.astype(BF)
     for s in range(2):
         for c in range(4):
-            rows = rows_ref[s, c]
-            left_ref[s, c] = dot(left_pick, rows).astype(BF)
-            right_ref[s, c] = dot(right_pick, rows).astype(BF)
+            left_ref[s, c] = dot(left_pick, rows_ref[s, c]).astype(BF)
     for copy in copies[2:]:
         copy.wait()
 
@@ -198,15 +196,15 @@
     high, low = inverse_tables(factor)
     vmem = pl.BlockSpec(memory_space=pltpu.VMEM)
     hbm = pl.BlockSpec(memory_space=pltpu.HBM)
-    rows = jax.ShapeDtypeStruct((2, 4, 256, COLS), BF)
+    left = jax.ShapeDtypeStruct((2, 4, 256, COLS), BF)
+    rows = jax.ShapeDtypeStruct((2, 4, 128, COLS), BF)
     table = jax.ShapeDtypeStruct((2 * F, LAGS), BF)
     return pl.pallas_call(
         gather_kernel,
         in_specs=[vmem, pl.BlockSpec(memory_space=pltpu.SMEM)] + [hbm] * 4,
         out_specs=[vmem] * 5,
-        out_shape=[rows, rows, jax.ShapeDtypeStruct((256, 128), BF), table, table],
+        out_shape=[left, rows, jax.ShapeDtypeStruct((256, 128 + REACH), BF), table, table],
         scratch_shapes=[
-            pltpu.VMEM((2, 4, 128, COLS), BF),
             pltpu.VMEM((1, 256), jnp.int32),
             pltpu.VMEM((1, 256), jnp.int32),
             pltpu.SemaphoreType.DMA((4,)),
@@ -216,18 +214,19 @@
     )(own, pair_count, *(in_hbm(x) for x in (pair_first.reshape(1, 256), pair_offset.reshape(1, 256), high, low)))
 
 
-def pairs_kernel(rim_ref, left_ref, right_ref, pick_ref, high_ref, low_ref, out_ref, rim_rows, parts_ref):
+def pairs_kernel(rim_ref, left_ref, own_ref, pick_ref, high_ref, low_ref, out_ref, rows_ref, parts_ref):
     apart = spread_matrix(8, True)
     for b in range(3):
         block = dot(apart, rim_ref[b * 8 : b * 8 + 8].reshape(128, COLS)).astype(BF)
         for c in range(4):
             for s in range(2):
                 at = (c * 2 + s) * 16
-                rim_rows[s, c, b * 16 : b * 16 + 16] = block[at : at + 16]
-    pick = pick_ref[:, :REACH]
+                rows_ref[s, c, 128 + b * 16 : 144 + b * 16] = block[at : at + 16]
+    rows_ref[:, :, :128] = own_ref[...]
+    pick = pick_ref[...]
 
     def right(s, c):
-        return right_ref[s, c].astype(F32) + dot(pick, rim_rows[s, c])
+        return dot(pick, rows_ref[s, c])
 
     for c in range(2):
         re = im = None
@@ -251,7 +250,7 @@
         in_specs=[vmem] * 6,
         out_specs=vmem,
         out_shape=jax.ShapeDtypeStruct((256, LAGS), BF),
-        scratch_shapes=[pltpu.VMEM((2, 4, REACH, COLS), BF), pltpu.VMEM((512, 2 * F), BF)],
+        scratch_shapes=[pltpu.VMEM((2, 4, 128 + REACH, COLS), BF), pltpu.VMEM((512, 2 * F), BF)],
         compiler_params=pltpu.CompilerParams(vmem_limit_bytes=32 * 1024 * 1024),
         name="pairs",
     )(rim, *parts)

time: 59.5 us -> 59.4 us (level)
  transfers between devices with their start and end apart: 1 -> 1, of which waited for: 1 -> 1; matrix products, arithmetic and copies ran while one was open for 0% -> 0% of each run, Pallas kernels for 3% -> 2%
where the time goes in v10:
time: 59.4 us; the launch traced here: 59.1 us
  blocking collectives  46.9 us (79%)
  Pallas kernels  5.65 us (10%)
  starting transfers between devices  3.07 us (5%)
  waiting for transfers between devices  2.19 us (4%)
  between operations  0.68 us (1%)
  other arithmetic  0.63 us (1%)
    all_to_all x1, blocking collectives, on_device(): own = lax.all_to_all(sent, 'chan', split_axis=0, concat_axis=0, tiled=True)  30.7 us
    all_to_all x1, blocking collectives, on_device(): lax.all_to_all(lags.reshape(groups, 256 // groups, LAGS), 'seg', 0, 0, ti...  16.2 us
    pallas_call x1, Pallas kernels, whitened(): pl.pallas_call(whiten_kernel, in_specs=[hbm] * 3, out_specs=pl.BlockSpec(...  3.16 us
    ppermute x1, starting transfers between devices, on_device(): lax.ppermute(own[:REACH // 2], 'chan', [(i + 1, i) for i in range(blocks...  3.07 us
    ppermute x1, waiting for transfers between devices, on_device(): lax.ppermute(own[:REACH // 2], 'chan', [(i + 1, i) for i in range(blocks...  2.19 us
    pallas_call x1, Pallas kernels, gathered(): pl.pallas_call(gather_kernel, in_specs=[vmem, pl.BlockSpec(memory_space=p...  1.28 us
    pallas_call x1, Pallas kernels, pair_lags(): pl.pallas_call(pairs_kernel, in_specs=[vmem] * 6, out_specs=vmem, out_sha...  1.2 us
  transfers between devices with their start and end apart: 1, of which 1 were waited for; matrix products, arithmetic and copies ran while one was open for 0% of the time, Pallas kernels for 2%

profile of v10, /device:TPU:5, one launch (start us, length us, event | category | flops | bytes accessed | tf_op | source)
XLA Modules:
  0.0 59.1 jit_solution(12694042794356993121)
XLA Ops:
  0.0 3.2 %whiten.1 = bf16[64,16,256]{2,1,0:T(8,128)(2,1)S(1)} custom-call(bf16[2,128,1536]{2,1,0:T(8,128)(2,1)} %raw_hbm.1, s32[1,128]{1,0:T(1,128)} %bitcast.7, bf16[384,1024]{1,0:T(8,128)(2,1)} %constant.8.clone.table_hbm), custom_call_target="tpu_custom_call" | custom-call | tf_op jit(solution)/shard_map/whiten/pallas_call | solution.py:144
  3.2 30.7 %all_to_all.10.own_ref = bf16[64,16,256]{2,1,0:T(8,128)(2,1)S(1)} all-to-all(bf16[64,16,256]{2,1,0:T(8,128)(2,1)S(1)} %whiten.1), channel_id=1, replica_groups=mesh['chan'=64,'seg'=8] {'chan'}, dimensions={0} | all-to-all | bytes 1048576 | tf_op jit(solution)/shard_map/all_to_all | solution.py:264
  33.9 3.1 %collective-permute-start = (bf16[24,16,256]{2,1,0:T(8,128)(2,1)S(1)}, bf16[24,16,256]{2,1,0:T(8,128)(2,1)S(1)}, u32[]{:S(2)}, u32[]{:S(2)}) collective-permute-start(bf16[24,16,256]{2,1,0:T(8,128)(2,1)S(1)} %slice.4), channel_id=1, source_target_pairs={{8,0},{16,8},{24,16},{32,24},{40,32},{48,40},{56,48},{64,56},{72,6... | collective-permute-start | bytes 589832 | tf_op jit(solution)/shard_map/ppermute | solution.py:265
  37.6 1.3 %gather.1 = (bf16[2,4,256,256]{3,2,1,0:T(8,128)(2,1)S(1)}, bf16[2,4,128,256]{3,2,1,0:T(8,128)(2,1)S(1)}, bf16[256,176]{1,0:T(8,128)(2,1)S(1)}, bf16[1024,256]{1,0:T(8,128)(2,1)S(1)}, bf16[1024,256]{1,0:T(8,128)(2,1)S(1)}) custom-call(bf16[64,16,256]{2,1,0:T(8,128)(2,1)S(1)} %all_to_all.10.own_ref, s32[1]{0:T(128)S(6)} %copy.9.count_ref, s32[1,256]{1,0:T(1,128)} %bitcast.5, ...), custom_call_target="tpu_custom_call" | custom-call | tf_op jit(solution)/shard_map/gather/pallas_call | solution.py:202
  38.9 2.2 %collective-permute-done.rim_ref = bf16[24,16,256]{2,1,0:T(8,128)(2,1)S(1)} collective-permute-done((bf16[24,16,256]{2,1,0:T(8,128)(2,1)S(1)}, bf16[24,16,256]{2,1,0:T(8,128)(2,1)S(1)}, u32[]{:S(2)}, u32[]{:S(2)}) %collective-permute-start) | collective-permute-done | bytes 196640 | tf_op jit(solution)/shard_map/ppermute | solution.py:265
  41.1 1.2 %pairs.1 = bf16[256,256]{1,0:T(8,128)(2,1)S(1)} custom-call(bf16[24,16,256]{2,1,0:T(8,128)(2,1)S(1)} %collective-permute-done.rim_ref, bf16[2,4,256,256]{3,2,1,0:T(8,128)(2,1)S(1)} %get-tuple-element.10.left_ref, bf16[2,4,128,256]{3,2,1,0:T(8,128)(2,1)S(1)} %get-tuple-element.11.own_ref, bf16[256,176]{1,0:T(8,128)(2,1)S(1)} %get-tuple-element.12.pick_ref, ...), custom_call_target="tpu_custom_call" | custom-call | tf_op jit(solution)/shard_map/pairs/pallas_call | solution.py:248
  42.3 16.2 %all_to_all.11 = bf16[8,32,256]{2,1,0:T(8,128)(2,1)S(1)} all-to-all(bf16[8,32,256]{2,1,0:T(8,128)(2,1)S(1)} %bitcast.4), channel_id=1, replica_groups=mesh['chan'=64,'seg'=8] {'seg'}, dimensions={0} | all-to-all | bytes 262144 | tf_op jit(solution)/shard_map/all_to_all | solution.py:268
  58.5 0.6 %convert_reduce_fusion = f32[32,256]{1,0:T(8,128)} fusion(bf16[8,32,256]{2,1,0:T(8,128)(2,1)S(1)} %all_to_all.11), kind=kLoop, calls=%fused_computation | loop fusion | flops 122880 | bytes 163840 | tf_op jit(solution)/shard_map/reduce_sum | solution.py:269
  (1 shorter events, 0.0 us)
Async XLA Ops:
  33.9 7.2 %collective-permute-start = (bf16[24,16,256]{2,1,0:T(8,128)(2,1)S(1)}, bf16[24,16,256]{2,1,0:T(8,128)(2,1)S(1)}, u32[]{:S(2)}, u32[]{:S(2)}) collective-permute-start(bf16[24,16,256]{2,1,0:T(8,128)(2,1)S(1)} %slice.4), channel_id=1, source_target_pairs={{8,0},{16,8},{24,16},{32,24},{40,32},{48,40},{56,48},{64,56},{72,6... | collective-permute-start | bytes 589832 | tf_op jit(solution)/shard_map/ppermute | solution.py:265

commit v11 on v10

--- a/solution.py
+++ b/solution.py
@@ -187,7 +187,7 @@
     pick_ref[...] = (any_at == second).astype(F32).T.astype(BF)
     for s in range(2):
         for c in range(4):
-            left_ref[s, c] = dot(left_pick, rows_ref[s, c]).astype(BF)
+            left_ref[s, c] = dot(left_pick, rows_ref[s, c])
     for copy in copies[2:]:
         copy.wait()
 
@@ -196,7 +196,7 @@
     high, low = inverse_tables(factor)
     vmem = pl.BlockSpec(memory_space=pltpu.VMEM)
     hbm = pl.BlockSpec(memory_space=pltpu.HBM)
-    left = jax.ShapeDtypeStruct((2, 4, 256, COLS), BF)
+    left = jax.ShapeDtypeStruct((2, 4, 256, COLS), F32)
     rows = jax.ShapeDtypeStruct((2, 4, 128, COLS), BF)
     table = jax.ShapeDtypeStruct((2 * F, LAGS), BF)
     return pl.pallas_call(
@@ -231,7 +231,7 @@
     for c in range(2):
         re = im = None
         for s in range(2):
-            a_re, a_im = left_ref[s, c].astype(F32), left_ref[s, c + 2].astype(F32)
+            a_re, a_im = left_ref[s, c], left_ref[s, c + 2]
             c_re, c_im = right(s, c), right(s, c + 2)
             one, two = a_re * c_re + a_im * c_im, a_im * c_re - a_re * c_im
             re = one if re is None else re + one

time: 59.4 us -> 59.3 us (level)
  no operation moved by 1% of the time
where the time goes in v11:
time: 59.3 us; the launch traced here: 59.1 us
  blocking collectives  46.9 us (79%)
  Pallas kernels  5.58 us (9%)
  starting transfers between devices  3.07 us (5%)
  waiting for transfers between devices  2.19 us (4%)
  between operations  0.68 us (1%)
  other arithmetic  0.63 us (1%)
    all_to_all x1, blocking collectives, on_device(): own = lax.all_to_all(sent, 'chan', split_axis=0, concat_axis=0, tiled=True)  30.7 us
    all_to_all x1, blocking collectives, on_device(): lax.all_to_all(lags.reshape(groups, 256 // groups, LAGS), 'seg', 0, 0, ti...  16.2 us
    pallas_call x1, Pallas kernels, whitened(): pl.pallas_call(whiten_kernel, in_specs=[hbm] * 3, out_specs=pl.BlockSpec(...  3.16 us
    ppermute x1, starting transfers between devices, on_device(): lax.ppermute(own[:REACH // 2], 'chan', [(i + 1, i) for i in range(blocks...  3.07 us
    ppermute x1, waiting for transfers between devices, on_device(): lax.ppermute(own[:REACH // 2], 'chan', [(i + 1, i) for i in range(blocks...  2.19 us
    pallas_call x1, Pallas kernels, gathered(): pl.pallas_call(gather_kernel, in_specs=[vmem, pl.BlockSpec(memory_space=p...  1.28 us
  transfers between devices with their start and end apart: 1, of which 1 were waited for; matrix products, arithmetic and copies ran while one was open for 0% of the time, Pallas kernels for 2%

profile of v11, /device:TPU:5, one launch (start us, length us, event | category | flops | bytes accessed | tf_op | source)
XLA Modules:
  0.0 59.1 jit_solution(7911546917294080824)
XLA Ops:
  0.0 3.2 %whiten.1 = bf16[64,16,256]{2,1,0:T(8,128)(2,1)S(1)} custom-call(bf16[2,128,1536]{2,1,0:T(8,128)(2,1)} %raw_hbm.1, s32[1,128]{1,0:T(1,128)} %bitcast.7, bf16[384,1024]{1,0:T(8,128)(2,1)} %constant.8.clone.table_hbm), custom_call_target="tpu_custom_call" | custom-call | tf_op jit(solution)/shard_map/whiten/pallas_call | solution.py:144
  3.2 30.7 %all_to_all.10.own_ref = bf16[64,16,256]{2,1,0:T(8,128)(2,1)S(1)} all-to-all(bf16[64,16,256]{2,1,0:T(8,128)(2,1)S(1)} %whiten.1), channel_id=1, replica_groups=mesh['chan'=64,'seg'=8] {'chan'}, dimensions={0} | all-to-all | bytes 1048576 | tf_op jit(solution)/shard_map/all_to_all | solution.py:264
  33.9 3.1 %collective-permute-start = (bf16[24,16,256]{2,1,0:T(8,128)(2,1)S(1)}, bf16[24,16,256]{2,1,0:T(8,128)(2,1)S(1)}, u32[]{:S(2)}, u32[]{:S(2)}) collective-permute-start(bf16[24,16,256]{2,1,0:T(8,128)(2,1)S(1)} %slice.4), channel_id=1, source_target_pairs={{8,0},{16,8},{24,16},{32,24},{40,32},{48,40},{56,48},{64,56},{72,6... | collective-permute-start | bytes 589832 | tf_op jit(solution)/shard_map/ppermute | solution.py:265
  37.6 1.3 %gather.1 = (f32[2,4,256,256]{3,2,1,0:T(8,128)S(1)}, bf16[2,4,128,256]{3,2,1,0:T(8,128)(2,1)S(1)}, bf16[256,176]{1,0:T(8,128)(2,1)S(1)}, bf16[1024,256]{1,0:T(8,128)(2,1)S(1)}, bf16[1024,256]{1,0:T(8,128)(2,1)S(1)}) custom-call(bf16[64,16,256]{2,1,0:T(8,128)(2,1)S(1)} %all_to_all.10.own_ref, s32[1]{0:T(128)S(6)} %copy.9.count_ref, s32[1,256]{1,0:T(1,128)} %bitcast.5, ...), custom_call_target="tpu_custom_call" | custom-call | tf_op jit(solution)/shard_map/gather/pallas_call | solution.py:202
  38.9 2.2 %collective-permute-done.rim_ref = bf16[24,16,256]{2,1,0:T(8,128)(2,1)S(1)} collective-permute-done((bf16[24,16,256]{2,1,0:T(8,128)(2,1)S(1)}, bf16[24,16,256]{2,1,0:T(8,128)(2,1)S(1)}, u32[]{:S(2)}, u32[]{:S(2)}) %collective-permute-start) | collective-permute-done | bytes 196640 | tf_op jit(solution)/shard_map/ppermute | solution.py:265
  41.1 1.1 %pairs.1 = bf16[256,256]{1,0:T(8,128)(2,1)S(1)} custom-call(bf16[24,16,256]{2,1,0:T(8,128)(2,1)S(1)} %collective-permute-done.rim_ref, f32[2,4,256,256]{3,2,1,0:T(8,128)S(1)} %get-tuple-element.10.left_ref, bf16[2,4,128,256]{3,2,1,0:T(8,128)(2,1)S(1)} %get-tuple-element.11.own_ref, bf16[256,176]{1,0:T(8,128)(2,1)S(1)} %get-tuple-element.12.pick_ref, ...), custom_call_target="tpu_custom_call" | custom-call | tf_op jit(solution)/shard_map/pairs/pallas_call | solution.py:248
  42.2 16.2 %all_to_all.11 = bf16[8,32,256]{2,1,0:T(8,128)(2,1)S(1)} all-to-all(bf16[8,32,256]{2,1,0:T(8,128)(2,1)S(1)} %bitcast.4), channel_id=1, replica_groups=mesh['chan'=64,'seg'=8] {'seg'}, dimensions={0} | all-to-all | bytes 262144 | tf_op jit(solution)/shard_map/all_to_all | solution.py:268
  58.4 0.6 %convert_reduce_fusion = f32[32,256]{1,0:T(8,128)} fusion(bf16[8,32,256]{2,1,0:T(8,128)(2,1)S(1)} %all_to_all.11), kind=kLoop, calls=%fused_computation | loop fusion | flops 122880 | bytes 163840 | tf_op jit(solution)/shard_map/reduce_sum | solution.py:269
  (1 shorter events, 0.0 us)
Async XLA Ops:
  33.9 7.2 %collective-permute-start = (bf16[24,16,256]{2,1,0:T(8,128)(2,1)S(1)}, bf16[24,16,256]{2,1,0:T(8,128)(2,1)S(1)}, u32[]{:S(2)}, u32[]{:S(2)}) collective-permute-start(bf16[24,16,256]{2,1,0:T(8,128)(2,1)S(1)} %slice.4), channel_id=1, source_target_pairs={{8,0},{16,8},{24,16},{32,24},{40,32},{48,40},{56,48},{64,56},{72,6... | collective-permute-start | bytes 589832 | tf_op jit(solution)/shard_map/ppermute | solution.py:265
